TPU v7x, 256 devices: a whole 4x4x8 slice. The times are simulated.
256 devices in a mesh: blk: 128 (over z, x, y_lo, core), seg: 2 (over y_hi).
Axes of the slice: x: 4, y: 4 (y_hi: 2, y_lo: 2; y = y_hi * 2 + y_lo), z: 8, core: 2. Of those that a mesh axis runs over, the one named last changes fastest.
Arguments:
- records: float32 [128, 60, 3, 3000], P('blk', 'seg')
- availability: int32 [128, 60], P('blk', 'seg'), may hold values from 0 to 1, as said below
Outputs:
- correlations: bfloat16 [128, 128, 9, 2048], P('blk', 'seg')
Inputs may be any that keep to these rules, and one draw needn't show every extreme that they name: `availability`: every station has at least one recorded segment.
All inputs are finite; a program needn't handle non-finite values.
Results may differ from a plain program's by a relative error of at most 0.0053.
Values may be sent and summed in bfloat16 or wider, within the bound.
A program may use at most 128 MiB of HBM per device.

v0:
```python
import math

import jax
import jax.numpy as jnp
from jax import lax
from jax.sharding import PartitionSpec as P

NFFT = 4096
FREQS = 512
WIDTH = 32
LAG = 1024


two_pi = 2.0 * math.pi


def forward_table(samples):
    times = lax.iota(jnp.int32, samples)
    bins = lax.iota(jnp.int32, FREQS) + 1
    phase = times[:, None] * bins[None, :] % NFFT
    angle = phase.astype(jnp.float32) * (two_pi / NFFT)
    return jnp.concatenate([jnp.cos(angle), -jnp.sin(angle)], axis=1)


def inverse_table():
    bins = lax.iota(jnp.int32, FREQS) + 1
    shifts = lax.iota(jnp.int32, 2 * LAG) - LAG + NFFT
    phase = bins[:, None] * shifts[None, :] % NFFT
    angle = phase.astype(jnp.float32) * (two_pi / NFFT)
    return jnp.concatenate([jnp.cos(angle), -jnp.sin(angle)], axis=0) * (2.0 / NFFT)


def cross_sum(left, right):
    return jnp.einsum("isak,jsbk->iajbk", left, right, preferred_element_type=jnp.float32)


def to_lags(stack, table):
    rows = stack.reshape(-1, 2 * FREQS)
    lagged = jnp.dot(
        rows, table, precision=lax.Precision.HIGHEST, preferred_element_type=jnp.float32
    )
    return lagged.reshape(stack.shape[0], stack.shape[1], stack.shape[2], 2 * LAG)


def body(records, availability):
    stations, seg_count, comps, samples = records.shape
    spectra = jnp.dot(
        records.reshape(-1, samples),
        forward_table(samples),
        precision=lax.Precision.HIGHEST,
        preferred_element_type=jnp.float32,
    )
    spectra = spectra.reshape(stations, seg_count, comps, 2 * FREQS)
    power = spectra[..., :FREQS] ** 2 + spectra[..., FREQS:] ** 2
    power = power.reshape(stations, seg_count, comps, FREQS // WIDTH, WIDTH)
    amplitude = jnp.sqrt(jnp.mean(power, axis=(2, 4)) + 1e-06)
    amplitude = jnp.repeat(amplitude, WIDTH, axis=2)
    present = availability.astype(jnp.float32)
    totals = lax.psum(jnp.sum(present, axis=1), "seg")
    weight = present / jnp.sqrt(totals)[:, None]
    factor = weight[:, :, None] / amplitude
    factor = jnp.concatenate([factor, factor], axis=-1)[:, :, None, :]
    white = (spectra * factor).astype(jnp.bfloat16)
    own_re = white[..., :FREQS]
    own_im = white[..., FREQS:]
    all_stations = stations * lax.axis_size("blk")
    piece = lax.all_gather(white, "blk", axis=0, tiled=True)
    far_re = piece[..., :FREQS]
    far_im = piece[..., FREQS:]
    real = cross_sum(own_re, far_re) + cross_sum(own_im, far_im)
    imag = cross_sum(own_im, far_re) - cross_sum(own_re, far_im)
    block = jnp.concatenate([real, imag], axis=-1)
    stack = block
    stack = jnp.transpose(stack, (0, 2, 1, 3, 4)).reshape(
        stations, all_stations, comps * comps, 2 * FREQS
    )
    table = inverse_table()
    summed = lax.psum_scatter(stack, "seg", scatter_dimension=1, tiled=True)
    mine = to_lags(summed, table)
    return mine.astype(jnp.bfloat16)


def solution(mesh):
    placed = (P("blk", "seg", None, None), P("blk", "seg"))
    return jax.shard_map(
        body, mesh=mesh, in_specs=placed, out_specs=P("blk", "seg", None, None), check_vma=False
    )
```

profile of v0, /device:TPU:1, one launch (start us, length us, event | category | flops | bytes accessed | tf_op | source)
XLA Modules:
  0.0 497.1 jit_solution(1804303317188322954)
XLA Ops:
  6.5 25.9 %fusion.22 = (f32[3000,512]{1,0:T(8,128)}, f32[3000,512]{1,0:T(8,128)}) fusion(s32[512]{0:T(512)S(1)} %iota_add_fusion.1), kind=kLoop, calls=%fused_computation.33 | loop fusion | flops 23040000 | bytes 12290048 | tf_op jit(solution)/shard_map/cos | solution.py:22
  32.4 3.2 reduce.4
  35.6 0.6 reshape.117
  36.2 10.4 %fusion.28 = f32[90,1024]{1,0:T(8,128)S(1)} fusion(f32[90,3000]{1,0:T(8,128)S(1)} %reshape.117, f32[3000,512]{1,0:T(8,128)} %get-tuple-element.10, f32[3000,512]{1,0:T(8,128)} %get-tuple-element.9), kind=kOutput, calls=%fused_computation.38 | convolution fusion | flops 3320832000 | bytes 13736640 | tf_op jit(solution)/shard_map/dot_general | solution.py:47
  46.6 0.2 reshape.118
  46.8 0.9 copy.21
  47.7 0.2 fusion.34
  47.9 0.1 reduce_sum.30
  48.0 0.1 reduce_sum.31
  48.2 0.1 broadcast_in_dim.4
  48.3 0.2 broadcast_in_dim.5
  48.5 0.6 convert_reduce_fusion
  49.1 6.7 %psum.7 = f32[1]{0:T(128)} all-reduce(f32[1]{0:T(128)} %bitcast.1), channel_id=1, replica_groups=mesh['blk'=128,'seg'=2] {'seg'}, use_global_device_ids=true, to_apply=%region_1.2 | all-reduce | flops 1 | bytes 8 | tf_op jit(solution)/shard_map/psum | solution.py:59
  56.5 0.1 broadcast_divide_fusion
  56.7 1.0 copy.28
  57.7 1.6 multiply_convert_fusion
  59.3 1.2 copy.22
  60.5 0.2 reduce-scatter.2.cloned.1.call-start
  60.8 246.3 %all-gather.2.cloned.1.call-done = bf16[128,30,3,1024]{3,1,2,0:T(8,128)(2,1)} async-done(((bf16[1,30,3,1024]{3,1,2,0:T(8,128)(2,1)}), bf16[128,30,3,1024]{3,1,2,0:T(8,128)(2,1)}) %all-gather.2.cloned.1.call-update) | async-done | bytes 23592976 | tf_op jit(solution)/shard_map/all_gather | solution.py:67
  307.0 18.0 %fusion.38 = (bf16[128,30,3,512]{3,1,2,0:T(8,128)(2,1)}, bf16[128,30,3,512]{3,1,2,0:T(8,128)(2,1)}) fusion(bf16[128,30,3,1024]{3,1,2,0:T(8,128)(2,1)} %all-gather.2.cloned.1.call-done), kind=kLoop, calls=%fused_computation.57 | loop fusion | bytes 47185920 | tf_op jit(solution)/shard_map/slice | solution.py:69
  325.1 17.9 %copy.30 = bf16[128,30,3,512]{0,1,2,3:T(8,128)(2,1)} copy(bf16[128,30,3,512]{3,1,2,0:T(8,128)(2,1)} %get-tuple-element.6) | data formatting | bytes 23592960
  343.0 8.5 %fusion.31 = f32[512,128,3,3]{1,3,2,0:T(4,128)} fusion(bf16[128,30,3,512]{0,1,2,3:T(8,128)(2,1)} %copy.30, bf16[1,30,3,1024]{1,2,3,0:T(4,128)(2,1)S(1)} %multiply_convert_fusion), kind=kOutput, calls=%fused_computation.41 | convolution fusion | flops 35389440 | bytes 14680064 | tf_op jit(solution)/shard_map/isak,jsbk->iajbk/dot_general | solution.py:34
  351.5 8.5 %fusion.32 = f32[512,128,3,3]{1,3,2,0:T(4,128)} fusion(bf16[128,30,3,512]{0,1,2,3:T(8,128)(2,1)} %copy.30, bf16[1,30,3,1024]{1,2,3,0:T(4,128)(2,1)S(1)} %multiply_convert_fusion), kind=kOutput, calls=%fused_computation.42 | convolution fusion | flops 35389440 | bytes 14680064 | tf_op jit(solution)/shard_map/isak,jsbk->iajbk/dot_general | solution.py:34
  360.0 17.9 %copy.31 = bf16[128,30,3,512]{0,1,2,3:T(8,128)(2,1)} copy(bf16[128,30,3,512]{3,1,2,0:T(8,128)(2,1)} %get-tuple-element.5) | data formatting | bytes 23592960
  377.9 6.8 %add_bitcast_fusion = f32[1,3,128,3,512]{2,1,3,4,0:T(4,128)S(1)} fusion(f32[512,128,3,3]{1,3,2,0:T(4,128)} %fusion.31, bf16[128,30,3,512]{0,1,2,3:T(8,128)(2,1)} %copy.31, bf16[1,30,3,1024]{1,2,3,0:T(4,128)(2,1)S(1)} %multiply_convert_fusion), kind=kOutput, calls=%fused_computation.31 | convolution fusion | flops 35979264 | bytes 17039360 | tf_op jit(solution)/shard_map/isak,jsbk->iajbk/dot_general | solution.py:34
  384.8 2.2 copy-done
  387.0 5.0 %subtract_bitcast_fusion = f32[1,3,128,3,512]{2,1,3,4,0:T(4,128)} fusion(f32[512,128,3,3]{1,3,2,0:T(4,128)} %fusion.32, bf16[128,30,3,512]{0,1,2,3:T(8,128)(2,1)S(1)} %copy-done, bf16[1,30,3,1024]{1,2,3,0:T(4,128)(2,1)S(1)} %multiply_convert_fusion), kind=kOutput, calls=%fused_computation.30 | convolution fusion | flops 35979264 | bytes 17825792 | tf_op jit(solution)/shard_map/isak,jsbk->iajbk/dot_general | solution.py:34
  392.0 5.9 %maximum_bitcast_fusion = f32[1,128,3,3,1024]{1,2,3,4,0:T(4,128)} fusion(f32[1,3,128,3,512]{2,1,3,4,0:T(4,128)} %subtract_bitcast_fusion, f32[1,3,128,3,512]{2,1,3,4,0:T(4,128)S(1)} %add_bitcast_fusion), kind=kLoop, calls=%fused_computation.15 | loop fusion | flops 1179648 | bytes 9437184 | tf_op jit(solution)/shard_map/transpose | solution.py:74
  397.9 7.0 %copy.25 = f32[1,128,3,3,1024]{4,1,3,2,0:T(8,128)} copy(f32[1,128,3,3,1024]{1,2,3,4,0:T(4,128)} %maximum_bitcast_fusion) | data formatting | bytes 9437184 | tf_op jit(solution)/shard_map/transpose | solution.py:74
  404.9 18.9 %fusion.27 = (f32[512,2048]{1,0:T(8,128)}, f32[512,2048]{1,0:T(8,128)}) fusion(s32[2048]{0:T(1024)S(1)} %iota_add_fusion, s32[512]{0:T(512)S(1)} %iota_add_fusion.1), kind=kLoop, calls=%fused_computation.36 | loop fusion | flops 15728640 | bytes 8398848 | tf_op jit(solution)/shard_map/cos | solution.py:30
  423.9 47.6 %reduce-scatter.2.cloned.1.call-done = f32[1,64,9,1024]{3,1,2,0:T(8,128)} async-done(((f32[1,128,9,1024]{3,1,2,0:T(8,128)}), f32[1,64,9,1024]{3,1,2,0:T(8,128)}) %reduce-scatter.2.cloned.1.call-update) | async-done | bytes 2359312 | tf_op jit(solution)/shard_map/reduce_scatter | solution.py:78
  471.4 18.9 %fusion.23 = bf16[1,64,9,2048]{3,1,2,0:T(8,128)(2,1)} fusion(f32[512,2048]{1,0:T(8,128)} %get-tuple-element.8, f32[512,2048]{1,0:T(8,128)} %get-tuple-element.7, f32[1,64,9,1024]{3,1,2,0:T(8,128)} %reduce-scatter.2.cloned.1.call-done), kind=kOutput, calls=%fused_computation.34 | convolution fusion | flops 14500888576 | bytes 13107200 | tf_op jit(solution)/shard_map/dot_general | solution.py:39
  (13 shorter events, 0.1 us)
Async XLA Ops:
  6.5 300.5 %all-gather.2.cloned.1.call-start = ((), (), s32[]{:S(2)}) async-start(), calls=%async_computation.1 | async-start | bytes 25362432 | tf_op jit(solution)/shard_map/all_gather | solution.py:67
  6.5 25.9 %copy-start.1 = (f32[1,30,3,3000]{3,0,2,1:T(1,128)S(1)}, f32[1,30,3,3000]{3,0,2,1:T(1,128)}, u32[]{:S(2)}) copy-start(f32[1,30,3,3000]{3,0,2,1:T(1,128)} %param.2) | copy-start | bytes 3240004
  46.6 1.9 copy-start.2
  60.5 410.9 %reduce-scatter.2.cloned.1.call-start = ((), (), s32[]{:S(2)}) async-start(), calls=%async_computation.2 | async-start | bytes 7077888 | tf_op jit(solution)/shard_map/reduce_scatter | solution.py:78
  377.9 9.1 %copy-start = (bf16[128,30,3,512]{0,1,2,3:T(8,128)(2,1)S(1)}, bf16[128,30,3,512]{0,1,2,3:T(8,128)(2,1)}, u32[]{:S(2)}) copy-start(bf16[128,30,3,512]{0,1,2,3:T(8,128)(2,1)} %copy.31) | copy-start | bytes 35389444
Sparse Core Ops, SparseCore 0:
  60.7 246.3 all-gather.1
  405.0 66.3 reduce-scatter.1
where the time goes:
time: 498 us; the launch traced here: 497 us
  waiting for transfers between devices  294 us (59%)
  local copies, waits for them, and re-layouts  67.4 us (14%)
  matrix products  58.2 us (12%)
  other arithmetic  56.6 us (11%)
  between operations  14.2 us (3%)
  blocking collectives  6.67 us (1%)
    all_gather x1, waiting for transfers between devices, body(): piece = lax.all_gather(white, 'blk', axis=0, tiled=True)  246 us
    reduce_scatter x1, waiting for transfers between devices, body(): summed = lax.psum_scatter(stack, 'seg', scatter_dimension=1, tiled=True)  47.6 us
    unnamed x8, local copies, waits for them, and re-layouts  38.1 us
    dot_general x4, matrix products, cross_sum(): jnp.einsum('isak,jsbk->iajbk', left, right, preferred_element_type=jnp.fl...  28.9 us
    cos x1, other arithmetic, forward_table(): return jnp.concatenate([jnp.cos(angle), -jnp.sin(angle)], axis=1)  25.9 us
    cos x1, other arithmetic, inverse_table(): jnp.cos(angle)  18.9 us
    dot_general x1, matrix products, to_lags(): jnp.dot(rows, table, precision=lax.Precision.HIGHEST, preferred_element_t...  18.9 us
    slice x1, local copies, waits for them, and re-layouts, body(): far_im = piece[..., FREQS:]  18 us
  transfers between devices with their start and end apart: 2, of which 2 were waited for; matrix products, arithmetic and copies ran while one was open for 4% of the time, Pallas kernels for 0%

commit v1 on v0

v1 whole, which is shorter than its diff:
```python
import functools
import math

import jax
import jax.numpy as jnp
import ml_dtypes
import numpy as np
from jax import lax
from jax.experimental import pallas as pl
from jax.experimental.pallas import tpu as pltpu
from jax.sharding import PartitionSpec as P

MESH = pl.DeviceIdType.MESH
F32 = jnp.float32
BF16 = jnp.bfloat16
NFFT = 4096
FREQS = 512
LAG = 1024
SEGS = 30
ROWS = 96
RESIDUES = ((1, 7), (2, 6), (3, 5), (8, 4))
HALF = math.sqrt(0.5)
NT = (((1,), (1,)), ((), ()))


def bin_of(p, f):
    return 16 * p + 8 * (f % 2) + np.array(RESIDUES)[f // 4, f // 2 % 2]


def forward_table():
    table = np.zeros((4, 32, 2, 2, 2, 2, 512))
    n = np.arange(512)
    for g in range(4):
        for which in range(2):
            for odd in range(2):
                k = 16 * np.arange(32) + 8 * odd + RESIDUES[g][which]
                angle = (k[:, None] * n[None, :] % NFFT) * (2 * np.pi / NFFT)
                cos, sin = np.cos(angle), np.sin(angle)
                if g == 3:
                    table[g, :, which, odd, 0, which] = cos
                    table[g, :, which, odd, 1, which] = -sin
                else:
                    sign = 1 - 2 * which
                    table[g, :, which, odd, 0, 0] = cos
                    table[g, :, which, odd, 0, 1] = sign * sin
                    table[g, :, which, odd, 1, 0] = -sin
                    table[g, :, which, odd, 1, 1] = sign * cos
    table = table.reshape(4, 256, 1024)
    high = table.astype(ml_dtypes.bfloat16)
    low = (table - high.astype(np.float64)).astype(ml_dtypes.bfloat16)
    return high, low


def inverse_table():
    p, f = np.meshgrid(np.arange(32), np.arange(16), indexing="ij")
    k = bin_of(p, f).reshape(-1)
    tau = np.arange(2 * LAG) - LAG
    angle = (k[:, None] * tau[None, :] % NFFT) * (2 * np.pi / NFFT)
    table = np.concatenate([np.cos(angle), -np.sin(angle)], axis=0) * (2.0 / NFFT)
    return table.astype(ml_dtypes.bfloat16)


def place_table():
    plain = np.zeros((2, 2, 128, 3, 128))
    turned = np.zeros((2, 2, 128, 3, 128))
    for seg in range(2):
        for s in range(SEGS):
            for c in range(3):
                for part in range(2):
                    plain[seg, part, 3 * s + c, c, 64 * part + 30 * seg + s] = 1
                turned[seg, 1, 3 * s + c, c, 30 * seg + s] = 1
                turned[seg, 0, 3 * s + c, c, 64 + 30 * seg + s] = -1
    both = np.stack([plain, turned]).reshape(2, 512, 384)
    return both.astype(ml_dtypes.bfloat16)


def place():
    blk, seg = lax.axis_index("blk"), lax.axis_index("seg")
    z, rest = blk // 16, blk % 16
    return z, rest // 4, seg * 2 + rest // 2 % 2, rest % 2, seg


def device(z, x, y, core):
    return (z * 16 + x * 4 + y % 2 * 2 + core, y // 2)


def partner(t, x, y, core):
    return (x + 2 + t // 8) % 4, (y + 2 + t // 2 % 4) % 4, (core + 1 + t) % 2


def spread(av):
    column = lax.broadcasted_iota(jnp.int32, (SEGS, 128), 1)
    row = lax.broadcasted_iota(jnp.int32, (SEGS, 128), 0)
    pick = ((column >= 3 * row) & (column < 3 * row + 3)).astype(F32)
    return jnp.dot(jnp.broadcast_to(av, (8, SEGS)), pick, preferred_element_type=F32)


def split_rows(w_ref, g, half, value):
    high = value.astype(BF16)
    low = (value - high.astype(F32)).astype(BF16)
    columns = pl.ds(512 * half, 512)
    w_ref[g, pl.ds(0, ROWS), columns] = high
    w_ref[g, pl.ds(128, ROWS), columns] = low


def stack_kernel(
    x_ref, av_ref, high_ref, low_ref, place_ref, out_ref,
    w, xs, white, rin, turn, gathered, left, stage, send, counts,
    count_sem, in_sem, ring_send, ring_recv, out_sem, own_sem,
):
    z, x, y, core, seg = place()
    slot = (x * 4 + y % 2 * 2 + core) * 2 + seg
    up, down = (z + 1) % 8, (z + 7) % 8
    barrier = pltpu.get_barrier_semaphore()

    def greet(t, carry):
        px, py, pc = partner(t, x, y, core)
        pl.semaphore_signal(barrier, inc=1, device_id=device(z, px, py, pc), device_id_type=MESH)
        return carry

    lax.fori_loop(0, 21, greet, 0)
    lax.fori_loop(22, 32, greet, 0)
    for other in (up, down):
        pl.semaphore_signal(barrier, inc=1, device_id=device(other, x, y, core), device_id_type=MESH)

    own = spread(av_ref[...].astype(F32))
    counts[0] = own
    part = [x_ref[:, 512 * n : 512 * (n + 1)] for n in range(6)]
    for g in range(4):
        for start in (ROWS, 128 + ROWS):
            w[g, pl.ds(start, 32), :] = jnp.zeros((32, 1024), BF16)
    d04 = part[0] - part[4]
    d13, s13 = part[1] - part[3], part[1] + part[3]
    split_rows(w, 0, 0, d04 + (d13 - part[5]) * HALF)
    split_rows(w, 0, 1, (part[5] - s13) * HALF - part[2])
    split_rows(w, 1, 0, part[0] + part[4] - part[2])
    split_rows(w, 1, 1, part[3] - part[1] - part[5])
    split_rows(w, 2, 0, d04 + (part[5] - d13) * HALF)
    split_rows(w, 2, 1, (part[5] - s13) * HALF + part[2])
    even, odd = part[0] + part[2] + part[4], s13 + part[5]
    split_rows(w, 3, 0, even + odd)
    split_rows(w, 3, 1, even - odd)

    pl.semaphore_wait(barrier, 33)
    count_copy = pltpu.make_async_remote_copy(
        src_ref=counts.at[0], dst_ref=counts.at[1], send_sem=count_sem.at[0], recv_sem=count_sem.at[1],
        device_id=device(z, x, (y + 2) % 4, core), device_id_type=MESH,
    )
    count_copy.start()

    power = jnp.zeros((32, 8, 128), F32)
    for g in range(4):
        high = lax.dot_general(high_ref[g], w[g], NT, preferred_element_type=F32)
        low = lax.dot_general(low_ref[g], w[g], NT, preferred_element_type=F32)
        both = high + low
        value = (both[:, :128] + both[:, 128:]).reshape(32, 8, 128)
        xs[:, pl.ds(8 * g, 8), :] = value
        power = power + value * value
    power = jnp.sum(power.reshape(16, 16, 128), axis=1)
    triple = power + pltpu.roll(power, 127, 1) + pltpu.roll(power, 126, 1)
    phase = lax.broadcasted_iota(jnp.int32, (16, 128), 1) % 3
    total = jnp.where(phase == 0, triple, jnp.where(phase == 1, pltpu.roll(triple, 1, 1), pltpu.roll(triple, 2, 1)))
    amplitude = jnp.sqrt(total * (1.0 / 96) + 1e-06)
    count_copy.wait()
    count = (jnp.sum(own, axis=1, keepdims=True) + jnp.sum(counts[1], axis=1, keepdims=True)) * (1.0 / 3)
    weight = own / jnp.sqrt(jnp.round(count))
    factor = weight[0:1] / amplitude
    white[...] = (xs[...].reshape(16, 64, 128) * factor[:, None, :]).reshape(32, 32, 128).astype(BF16)

    def scatter(t, carry):
        px, py, pc = partner(t, x, y, core)
        target = (px * 4 + py % 2 * 2 + pc) * 2 + py // 2
        pltpu.make_async_remote_copy(
            src_ref=white.at[target], dst_ref=rin.at[slot], send_sem=in_sem.at[0], recv_sem=in_sem.at[1],
            device_id=device(z, px, py, pc), device_id_type=MESH,
        ).start()
        return carry

    lax.fori_loop(0, 21, scatter, 0)
    lax.fori_loop(22, 32, scatter, 0)
    pltpu.make_async_copy(rin.at[pl.ds(0, 31)], rin.at[pl.ds(0, 31)], in_sem.at[1]).wait()
    rin[slot] = white[slot]

    def swap(source, carry):
        start = source % 2 * 512 + source // 2
        turn[pl.ds(start, 32, stride=16), :] = rin[source].astype(F32)
        return carry

    lax.fori_loop(0, 32, swap, 0)
    pieces = turn[...].reshape(2, 16, 2, 16, 128)
    rows = jnp.concatenate(
        [pieces[s, :, part].reshape(256, 128).astype(BF16) for s in range(2) for part in range(2)], axis=1
    )
    plain = jnp.dot(rows, place_ref[0], preferred_element_type=F32).astype(BF16)
    turned = jnp.dot(rows, place_ref[1], preferred_element_type=F32).astype(BF16)
    for c in range(3):
        one = plain[:, 128 * c : 128 * (c + 1)].reshape(16, 16, 128)
        gathered[c, z] = one
        left[:, pl.ds(16 * c, 16), :] = one
        left[:, pl.ds(48 + 16 * c, 16), :] = turned[:, 128 * c : 128 * (c + 1)].reshape(16, 16, 128)

    def pass_on(c, hop, way, start):
        source = (z + 9 - hop) % 8 if way == 0 else (z + hop - 1) % 8
        copy = pltpu.make_async_remote_copy(
            src_ref=gathered.at[c, source], dst_ref=gathered.at[c, source],
            send_sem=ring_send.at[c, hop - 1, way], recv_sem=ring_recv.at[c, hop - 1, way],
            device_id=device(up if way == 0 else down, x, y, core), device_id_type=MESH,
        )
        if start:
            copy.start()
        return copy

    def last_hop(c, start):
        source = (z + 5 + 6 * core) % 8
        copy = pltpu.make_async_remote_copy(
            src_ref=gathered.at[c, source], dst_ref=gathered.at[c, source],
            send_sem=ring_send.at[c, 3, 0], recv_sem=ring_recv.at[c, 3, 0],
            device_id=device((z + 1 + 6 * core) % 8, x, y, core), device_id_type=MESH,
        )
        if start:
            copy.start()
        return copy

    def arrive(c, hop):
        if hop == 4:
            last_hop(c, False).wait_recv()
        else:
            for way in range(2):
                pass_on(c, hop, way, False).wait_recv()

    def forward(c, hop):
        if hop == 4:
            last_hop(c, True)
        else:
            for way in range(2):
                pass_on(c, hop, way, True)

    lane = lax.broadcasted_iota(jnp.int32, (16, 128), 1) < 64

    def cross(b):
        def one_bin(f, carry):
            right = gathered[b, :, f].reshape(128, 128)
            product = lax.dot_general(left[f], right, NT, preferred_element_type=F32)
            for a in range(3):
                re = product[16 * a : 16 * (a + 1)]
                im = product[48 + 16 * a : 48 + 16 * (a + 1)]
                mixed = pltpu.roll(jnp.where(lane, im, re), 64, 1)
                stage[pl.ds(512 * a + f, 16, stride=16), :] = jnp.where(lane, re, mixed)
                stage[pl.ds(512 * a + 256 + f, 16, stride=16), :] = jnp.where(lane, mixed, im)
            return carry

        lax.fori_loop(0, 16, one_bin, 0)
        send[b] = jnp.stack([stage[pl.ds(512 * a, 512), :].reshape(2, 16, 16, 128).astype(BF16) for a in range(3)], axis=2)

        def scatter(t, carry):
            px, py, pc = partner(t, x, y, core)
            pltpu.make_async_remote_copy(
                src_ref=send.at[b, py // 2, px * 4 + py % 2 * 2 + pc], dst_ref=out_ref.at[b, slot],
                send_sem=out_sem.at[b, 0], recv_sem=out_sem.at[b, 1],
                device_id=device(z, px, py, pc), device_id_type=MESH,
            ).start()
            return carry

        lax.fori_loop(0, 21, scatter, 0)
        lax.fori_loop(22, 32, scatter, 0)
        pltpu.make_async_copy(send.at[b, seg, slot // 2], out_ref.at[b, slot], own_sem.at[b]).start()

    forward(0, 1)
    forward(1, 1)
    forward(2, 1)
    for hop in range(1, 4):
        for c in range(3):
            arrive(c, hop)
            forward(c, hop + 1)
    for c in range(3):
        arrive(c, 4)
        cross(c)

    pltpu.make_async_copy(white.at[pl.ds(0, 31)], white.at[pl.ds(0, 31)], in_sem.at[0]).wait()
    for c in range(3):
        for hop in range(1, 4):
            for way in range(2):
                pass_on(c, hop, way, False).wait_send()
        last_hop(c, False).wait_send()
    for b in range(3):
        pltpu.make_async_copy(send.at[b, seg, slot // 2], out_ref.at[b, slot], own_sem.at[b]).wait()
        whole = out_ref.at[b, pl.ds(0, 31)]
        pltpu.make_async_copy(whole, whole, out_sem.at[b, 1]).wait()
        pltpu.make_async_copy(whole, whole, out_sem.at[b, 0]).wait()


def stacked(records, availability, high, low, places):
    vmem = pl.BlockSpec(memory_space=pltpu.VMEM)
    return pl.pallas_call(
        stack_kernel,
        name="stack",
        out_shape=jax.ShapeDtypeStruct((3, 32, 3, 16, 128), BF16),
        in_specs=[vmem] * 5,
        out_specs=pl.BlockSpec(memory_space=pl.ANY),
        scratch_shapes=[
            pltpu.VMEM((4, 256, 1024), BF16),
            pltpu.VMEM((32, 32, 128), F32),
            pltpu.VMEM((32, 32, 128), BF16),
            pltpu.VMEM((32, 32, 128), BF16),
            pltpu.VMEM((1024, 128), F32),
            pltpu.VMEM((3, 8, 16, 16, 128), BF16),
            pltpu.VMEM((16, 96, 128), BF16),
            pltpu.VMEM((1536, 128), F32),
            pltpu.VMEM((3, 2, 16, 3, 16, 128), BF16),
            pltpu.VMEM((2, 8, 128), F32),
            pltpu.SemaphoreType.DMA((2,)),
            pltpu.SemaphoreType.DMA((2,)),
            pltpu.SemaphoreType.DMA((3, 4, 2)),
            pltpu.SemaphoreType.DMA((3, 4, 2)),
            pltpu.SemaphoreType.DMA((3, 2)),
            pltpu.SemaphoreType.DMA((3,)),
        ],
        compiler_params=pltpu.CompilerParams(
            collective_id=0, has_side_effects=True, vmem_limit_bytes=48 << 20
        ),
    )(records, availability, high, low, places)


def lag_kernel(s_ref, t_ref, out_ref, rows):
    @pl.when(pl.program_id(0) == 0)
    def _():
        for a in range(3):
            for b in range(3):
                block = s_ref[b, :, a].reshape(512, 128).T
                first = 64 * (3 * a + b)
                rows[pl.ds(first, 64), pl.ds(0, 512)] = block[:64]
                rows[pl.ds(first, 64), pl.ds(512, 512)] = block[64:]

    lagged = jnp.dot(rows[...], t_ref[...], preferred_element_type=F32)
    out_ref[...] = lagged.astype(BF16).reshape(9, 64, lagged.shape[1])


def to_lags(stack, table):
    width = 512
    return pl.pallas_call(
        lag_kernel,
        name="lags",
        grid=(2 * LAG // width,),
        out_shape=jax.ShapeDtypeStruct((9, 64, 2 * LAG), BF16),
        in_specs=[
            pl.BlockSpec((3, 32, 3, 16, 128), lambda n: (0, 0, 0, 0, 0)),
            pl.BlockSpec((1024, width), lambda n: (0, n)),
        ],
        out_specs=pl.BlockSpec((9, 64, width), lambda n: (0, 0, n)),
        scratch_shapes=[pltpu.VMEM((576, 1024), BF16)],
        compiler_params=pltpu.CompilerParams(vmem_limit_bytes=40 << 20),
    )(stack, table)


def body(records, availability):
    high, low = forward_table()
    samples = records.shape[-1]
    x = jnp.pad(records.reshape(90, samples), ((0, ROWS - 90), (0, 3072 - samples)))
    stack = stacked(x, availability, jnp.asarray(high), jnp.asarray(low), jnp.asarray(place_table()))
    lagged = to_lags(stack, jnp.asarray(inverse_table()))
    return jnp.transpose(lagged, (1, 0, 2))[None]


def solution(mesh):
    placed = (P("blk", "seg", None, None), P("blk", "seg"))
    return jax.shard_map(
        body, mesh=mesh, in_specs=placed, out_specs=P("blk", "seg", None, None), check_vma=False
    )
```

time: 498 us -> 70.6 us (0.14)
  waiting for transfers between devices: 294 us -> 0 us
  local copies, waits for them, and re-layouts: 67.4 us -> 2.2 us
  Pallas kernels: 0 us -> 64 us
  matrix products: 58.2 us -> 0 us
  other arithmetic: 56.6 us -> 4.25 us
  between operations: 14.2 us -> 0.06 us
  blocking collectives: 6.67 us -> 0 us
    all_gather x1 -> x0, waiting for transfers between devices: 246 us -> none  [body(): piece = lax.all_gather(white, 'blk', axis=0, tiled=True)]
    pallas_call x0 -> x2, Pallas kernels: none -> 64 us  [the longest x1 59.3 us: stacked(): pl.pallas_call(stack_kernel, name='stack', out_shape=jax.ShapeDtypeStruct...]
    dot_general x6 -> x0, matrix products: 58.2 us -> none  [the longest x4 28.9 us: cross_sum(): jnp.einsum('isak,jsbk->iajbk', left, right, preferred_element_type=jnp.fl...]
    reduce_scatter x1 -> x0, waiting for transfers between devices: 47.6 us -> none  [body(): summed = lax.psum_scatter(stack, 'seg', scatter_dimension=1, tiled=True)]
    cos x2 -> x0, other arithmetic: 44.8 us -> none  [the longest x1 25.9 us: forward_table(): return jnp.concatenate([jnp.cos(angle), -jnp.sin(angle)], axis=1)]
    unnamed x8, local copies, waits for them, and re-layouts: 38.1 us -> 1.55 us
    slice x1 -> x0, local copies, waits for them, and re-layouts: 18 us -> none  [body(): far_im = piece[..., FREQS:]]
    transpose x1 -> x0, local copies, waits for them, and re-layouts: 6.97 us -> none  [body(): jnp.transpose(stack, (0, 2, 1, 3, 4))]
  transfers between devices with their start and end apart: 2 -> 0, of which waited for: 2 -> 0; matrix products, arithmetic and copies ran while one was open for 4% -> 0% of each run, Pallas kernels for 0% -> 0%
where the time goes in v1:
time: 70.6 us; the launch traced here: 70.5 us
  Pallas kernels  64 us (91%)
  other arithmetic  4.25 us (6%)
  local copies, waits for them, and re-layouts  2.2 us (3%)
    pallas_call x1, Pallas kernels, stacked(): pl.pallas_call(stack_kernel, name='stack', out_shape=jax.ShapeDtypeStruct...  59.3 us
    pallas_call x1, Pallas kernels, to_lags(): pl.pallas_call(lag_kernel, name='lags', grid=(2 * LAG // width,), out_sha...  4.67 us
    unnamed x1, other arithmetic  4.25 us
    unnamed x8, local copies, waits for them, and re-layouts  1.55 us

profile of v1, /device:TPU:1, one launch (start us, length us, event | category | flops | bytes accessed | tf_op | source)
XLA Modules:
  0.0 70.5 jit_solution(8972952130485688169)
XLA Ops:
  0.0 4.3 %reduce = f32[30,3,3000]{2,1,0:T(4,128)S(1)} reduce(f32[1,30,3,3000]{3,0,2,1:T(1,128)} %param.6, f32[]{:T(128)} %constant.19), dimensions={0}, to_apply=%param.6.reduce_sub_computation | reduce | bytes 2160004 | tf_op args[0]
  4.3 0.0 copy-start.2
  4.3 0.6 reshape.3
  4.8 0.0 copy-start.1
  4.8 0.0 copy-start.3
  4.9 0.1 pad.4.x_ref
  5.0 0.4 copy-done.2
  5.4 1.1 %copy-done.1 = bf16[4,256,1024]{2,1,0:T(8,128)(2,1)S(1)} copy-done((bf16[4,256,1024]{2,1,0:T(8,128)(2,1)S(1)}, bf16[4,256,1024]{2,1,0:T(8,128)(2,1)}, u32[]{:S(2)}) %copy-start.1) | copy-done | bytes 2097176
  6.5 0.0 copy-done.3
  6.5 0.0 copy-start
  6.5 59.3 %stack.1.s_ref = bf16[3,32,3,16,128]{4,3,2,1,0:T(8,128)(2,1)S(1)} custom-call(f32[96,3072]{1,0:T(8,128)S(1)} %pad.4.x_ref, s32[1,30]{1,0:T(1,128)S(1)} %copy-done.3, bf16[4,256,1024]{2,1,0:T(8,128)(2,1)S(1)} %copy-done.1, bf16[4,256,1024]{2,1,0:T(8,128)(2,1)} %constant.12.clone.low_ref, bf16[2,512,384]{2,1,0:T(8,128)(2,1)S(1)} %copy-done.2), custom_call_target="tpu_custom_call" | custom-call | tf_op jit(solution)/shard_map/stack/pallas_call | solution.py:294
  65.8 0.0 copy-done
  65.8 4.7 %lags.1 = bf16[9,64,2048]{2,1,0:T(8,128)(2,1)} custom-call(bf16[3,32,3,16,128]{4,3,2,1,0:T(8,128)(2,1)S(1)} %stack.1.s_ref, bf16[1024,2048]{1,0:T(8,128)(2,1)S(1)} %copy-done), custom_call_target="tpu_custom_call" | custom-call | tf_op jit(solution)/shard_map/lags/pallas_call | solution.py:340
Async XLA Ops:
  4.3 1.1 %copy-start.2 = (bf16[2,512,384]{2,1,0:T(8,128)(2,1)S(1)}, bf16[2,512,384]{2,1,0:T(8,128)(2,1)}, u32[]{:S(2)}) copy-start(bf16[2,512,384]{2,1,0:T(8,128)(2,1)} %constant.13.clone.place_ref) | copy-start | bytes 2359300
  4.8 1.7 %copy-start.1 = (bf16[4,256,1024]{2,1,0:T(8,128)(2,1)S(1)}, bf16[4,256,1024]{2,1,0:T(8,128)(2,1)}, u32[]{:S(2)}) copy-start(bf16[4,256,1024]{2,1,0:T(8,128)(2,1)} %constant.11.clone.high_ref) | copy-start | bytes 6291460
  4.8 1.6 %copy-start.3 = (s32[1,30]{1,0:T(1,128)S(1)}, s32[1,30]{1,0:T(1,128)}, u32[]{:S(2)}) copy-start(s32[1,30]{1,0:T(1,128)} %av_ref.1) | copy-start | bytes 364
  6.5 59.3 %copy-start = (bf16[1024,2048]{1,0:T(8,128)(2,1)S(1)}, bf16[1024,2048]{1,0:T(8,128)(2,1)}, u32[]{:S(2)}) copy-start(bf16[1024,2048]{1,0:T(8,128)(2,1)} %constant.14.clone.t_ref) | copy-start | bytes 12582916

commit v2 on v1

--- a/solution.py
+++ b/solution.py
@@ -17,9 +17,13 @@
 FREQS = 512
 LAG = 1024
 SEGS = 30
-ROWS = 96
+ROWS = 90
 RESIDUES = ((1, 7), (2, 6), (3, 5), (8, 4))
 HALF = math.sqrt(0.5)
+SCHEDULE = (
+    "F01 F11 F21 A01 F02 A11 F12 A21 F22 A02 F03 A12 F13 A22 F23 "
+    "A03 F04 A13 F14 A23 F24 A04 X0 A14 X1 A24 X2"
+)
 NT = (((1,), (1,)), ((), ()))
 
 
@@ -104,31 +108,40 @@
 
 
 def stack_kernel(
-    x_ref, av_ref, high_ref, low_ref, place_ref, out_ref,
+    x_hbm, av_ref, high_hbm, low_hbm, place_hbm, out_ref,
+    x_ref, high_ref, low_ref, place_ref,
     w, xs, white, rin, turn, gathered, left, stage, send, counts,
-    count_sem, in_sem, ring_send, ring_recv, out_sem, own_sem,
+    load_sem, line_sem, core_sem, count_sem, in_sem, ring_send, ring_recv, out_sem, own_sem,
 ):
     z, x, y, core, seg = place()
     slot = (x * 4 + y % 2 * 2 + core) * 2 + seg
     up, down = (z + 1) % 8, (z + 7) % 8
     barrier = pltpu.get_barrier_semaphore()
 
-    def greet(t, carry):
-        px, py, pc = partner(t, x, y, core)
-        pl.semaphore_signal(barrier, inc=1, device_id=device(z, px, py, pc), device_id_type=MESH)
-        return carry
-
-    lax.fori_loop(0, 21, greet, 0)
-    lax.fori_loop(22, 32, greet, 0)
-    for other in (up, down):
-        pl.semaphore_signal(barrier, inc=1, device_id=device(other, x, y, core), device_id_type=MESH)
+    lines = [((x + n) % 4, y, core) for n in range(1, 4)]
+    near = [device(z, *at) for at in lines]
+    near += [device(z, x, (y + n) % 4, core) for n in range(1, 4)]
+    near += [device(z, x, y, 1 - core), device(up, x, y, core), device(down, x, y, core)]
+    for other in near:
+        pl.semaphore_signal(barrier, inc=1, device_id=other, device_id_type=MESH)
+
+    loads = [
+        pltpu.make_async_copy(source, target, load_sem.at[n])
+        for n, (source, target) in enumerate(
+            ((x_hbm, x_ref), (high_hbm, high_ref), (low_hbm, low_ref), (place_hbm, place_ref))
+        )
+    ]
+    for load in loads:
+        load.start()
 
     own = spread(av_ref[...].astype(F32))
     counts[0] = own
-    part = [x_ref[:, 512 * n : 512 * (n + 1)] for n in range(6)]
     for g in range(4):
-        for start in (ROWS, 128 + ROWS):
-            w[g, pl.ds(start, 32), :] = jnp.zeros((32, 1024), BF16)
+        for start in (80, 208):
+            w[g, pl.ds(start, 48), :] = jnp.zeros((48, 1024), BF16)
+    loads[0].wait()
+    part = [x_ref[:, 0, pl.ds(512 * n, 512)] for n in range(5)]
+    part.append(jnp.concatenate([x_ref[:, 0, pl.ds(2560, 440)], jnp.zeros((ROWS, 72), F32)], axis=1))
     d04 = part[0] - part[4]
     d13, s13 = part[1] - part[3], part[1] + part[3]
     split_rows(w, 0, 0, d04 + (d13 - part[5]) * HALF)
@@ -141,7 +154,9 @@
     split_rows(w, 3, 0, even + odd)
     split_rows(w, 3, 1, even - odd)
 
-    pl.semaphore_wait(barrier, 33)
+    pl.semaphore_wait(barrier, 9)
+    for at in lines:
+        pl.semaphore_signal(line_sem, inc=1, device_id=device(z, *at), device_id_type=MESH)
     count_copy = pltpu.make_async_remote_copy(
         src_ref=counts.at[0], dst_ref=counts.at[1], send_sem=count_sem.at[0], recv_sem=count_sem.at[1],
         device_id=device(z, x, (y + 2) % 4, core), device_id_type=MESH,
@@ -149,7 +164,12 @@
     count_copy.start()
 
     power = jnp.zeros((32, 8, 128), F32)
+    loads[1].wait()
+    loads[2].wait()
     for g in range(4):
+        if g == 2:
+            pl.semaphore_wait(line_sem, 3)
+            pl.semaphore_signal(core_sem, inc=1, device_id=device(z, x, y, 1 - core), device_id_type=MESH)
         high = lax.dot_general(high_ref[g], w[g], NT, preferred_element_type=F32)
         low = lax.dot_general(low_ref[g], w[g], NT, preferred_element_type=F32)
         both = high + low
@@ -167,6 +187,8 @@
     factor = weight[0:1] / amplitude
     white[...] = (xs[...].reshape(16, 64, 128) * factor[:, None, :]).reshape(32, 32, 128).astype(BF16)
 
+    pl.semaphore_wait(core_sem, 1)
+
     def scatter(t, carry):
         px, py, pc = partner(t, x, y, core)
         target = (px * 4 + py % 2 * 2 + pc) * 2 + py // 2
@@ -187,6 +209,7 @@
         return carry
 
     lax.fori_loop(0, 32, swap, 0)
+    loads[3].wait()
     pieces = turn[...].reshape(2, 16, 2, 16, 128)
     rows = jnp.concatenate(
         [pieces[s, :, part].reshape(256, 128).astype(BF16) for s in range(2) for part in range(2)], axis=1
@@ -238,18 +261,19 @@
     lane = lax.broadcasted_iota(jnp.int32, (16, 128), 1) < 64
 
     def cross(b):
-        def one_bin(f, carry):
-            right = gathered[b, :, f].reshape(128, 128)
-            product = lax.dot_general(left[f], right, NT, preferred_element_type=F32)
-            for a in range(3):
-                re = product[16 * a : 16 * (a + 1)]
-                im = product[48 + 16 * a : 48 + 16 * (a + 1)]
-                mixed = pltpu.roll(jnp.where(lane, im, re), 64, 1)
-                stage[pl.ds(512 * a + f, 16, stride=16), :] = jnp.where(lane, re, mixed)
-                stage[pl.ds(512 * a + 256 + f, 16, stride=16), :] = jnp.where(lane, mixed, im)
+        def four_bins(step, carry):
+            for f in [4 * step + n for n in range(4)]:
+                right = gathered[b, :, f].reshape(128, 128)
+                product = lax.dot_general(left[f], right, NT, preferred_element_type=F32)
+                for a in range(3):
+                    re = product[16 * a : 16 * (a + 1)]
+                    im = product[48 + 16 * a : 48 + 16 * (a + 1)]
+                    mixed = pltpu.roll(jnp.where(lane, im, re), 64, 1)
+                    stage[pl.ds(512 * a + f, 16, stride=16), :] = jnp.where(lane, re, mixed)
+                    stage[pl.ds(512 * a + 256 + f, 16, stride=16), :] = jnp.where(lane, mixed, im)
             return carry
 
-        lax.fori_loop(0, 16, one_bin, 0)
+        lax.fori_loop(0, 4, four_bins, 0)
         send[b] = jnp.stack([stage[pl.ds(512 * a, 512), :].reshape(2, 16, 16, 128).astype(BF16) for a in range(3)], axis=2)
 
         def scatter(t, carry):
@@ -265,16 +289,9 @@
         lax.fori_loop(22, 32, scatter, 0)
         pltpu.make_async_copy(send.at[b, seg, slot // 2], out_ref.at[b, slot], own_sem.at[b]).start()
 
-    forward(0, 1)
-    forward(1, 1)
-    forward(2, 1)
-    for hop in range(1, 4):
-        for c in range(3):
-            arrive(c, hop)
-            forward(c, hop + 1)
-    for c in range(3):
-        arrive(c, 4)
-        cross(c)
+    steps = {"F": forward, "A": arrive, "X": cross}
+    for step in SCHEDULE.split():
+        steps[step[0]](*(int(digit) for digit in step[1:]))
 
     pltpu.make_async_copy(white.at[pl.ds(0, 31)], white.at[pl.ds(0, 31)], in_sem.at[0]).wait()
     for c in range(3):
@@ -290,14 +307,18 @@
 
 
 def stacked(records, availability, high, low, places):
-    vmem = pl.BlockSpec(memory_space=pltpu.VMEM)
+    vmem, hbm = pl.BlockSpec(memory_space=pltpu.VMEM), pl.BlockSpec(memory_space=pl.ANY)
     return pl.pallas_call(
         stack_kernel,
         name="stack",
         out_shape=jax.ShapeDtypeStruct((3, 32, 3, 16, 128), BF16),
-        in_specs=[vmem] * 5,
-        out_specs=pl.BlockSpec(memory_space=pl.ANY),
+        in_specs=[hbm, vmem, hbm, hbm, hbm],
+        out_specs=hbm,
         scratch_shapes=[
+            pltpu.VMEM(records.shape, F32),
+            pltpu.VMEM(high.shape, BF16),
+            pltpu.VMEM(low.shape, BF16),
+            pltpu.VMEM(places.shape, BF16),
             pltpu.VMEM((4, 256, 1024), BF16),
             pltpu.VMEM((32, 32, 128), F32),
             pltpu.VMEM((32, 32, 128), BF16),
@@ -308,6 +329,9 @@
             pltpu.VMEM((1536, 128), F32),
             pltpu.VMEM((3, 2, 16, 3, 16, 128), BF16),
             pltpu.VMEM((2, 8, 128), F32),
+            pltpu.SemaphoreType.DMA((4,)),
+            pltpu.SemaphoreType.REGULAR,
+            pltpu.SemaphoreType.REGULAR,
             pltpu.SemaphoreType.DMA((2,)),
             pltpu.SemaphoreType.DMA((2,)),
             pltpu.SemaphoreType.DMA((3, 4, 2)),
@@ -316,7 +340,7 @@
             pltpu.SemaphoreType.DMA((3,)),
         ],
         compiler_params=pltpu.CompilerParams(
-            collective_id=0, has_side_effects=True, vmem_limit_bytes=48 << 20
+            collective_id=0, has_side_effects=True, vmem_limit_bytes=62 << 20
         ),
     )(records, availability, high, low, places)
 
@@ -348,14 +372,14 @@
         ],
         out_specs=pl.BlockSpec((9, 64, width), lambda n: (0, 0, n)),
         scratch_shapes=[pltpu.VMEM((576, 1024), BF16)],
-        compiler_params=pltpu.CompilerParams(vmem_limit_bytes=40 << 20),
+        compiler_params=pltpu.CompilerParams(vmem_limit_bytes=62 << 20),
     )(stack, table)
 
 
 def body(records, availability):
     high, low = forward_table()
     samples = records.shape[-1]
-    x = jnp.pad(records.reshape(90, samples), ((0, ROWS - 90), (0, 3072 - samples)))
+    x = records.reshape(ROWS, 1, samples)
     stack = stacked(x, availability, jnp.asarray(high), jnp.asarray(low), jnp.asarray(place_table()))
     lagged = to_lags(stack, jnp.asarray(inverse_table()))
     return jnp.transpose(lagged, (1, 0, 2))[None]

time: 70.6 us -> 59.3 us (0.84)
  Pallas kernels: 64 us -> 59.2 us
  other arithmetic: 4.25 us -> 0 us
  local copies, waits for them, and re-layouts: 2.2 us -> 0 us
    pallas_call x1, Pallas kernels: 59.3 us -> 52.5 us  [stacked(): pl.pallas_call(stack_kernel, name='stack', out_shape=jax.ShapeDtypeStruct...]
    unnamed x1 -> x0, other arithmetic: 4.25 us -> none
    pallas_call x1, Pallas kernels: 4.67 us -> 6.67 us  [to_lags(): pl.pallas_call(lag_kernel, name='lags', grid=(2 * LAG // width,), out_sha...]
    unnamed x8 -> x0, local copies, waits for them, and re-layouts: 1.55 us -> none
where the time goes in v2:
time: 59.3 us; the launch traced here: 59.2 us
  Pallas kernels  59.2 us (100%)
    pallas_call x1, Pallas kernels, stacked(): pl.pallas_call(stack_kernel, name='stack', out_shape=jax.ShapeDtypeStruct...  52.5 us
    pallas_call x1, Pallas kernels, to_lags(): pl.pallas_call(lag_kernel, name='lags', grid=(2 * LAG // width,), out_sha...  6.67 us

profile of v2, /device:TPU:1, one launch (start us, length us, event | category | flops | bytes accessed | tf_op | source)
XLA Modules:
  0.0 59.2 jit_solution(11842035677694105085)
XLA Ops:
  0.0 52.5 %stack.1.s_ref = bf16[3,32,3,16,128]{4,3,2,1,0:T(8,128)(2,1)} custom-call(f32[90,1,3000]{2,1,0:T(1,128)} %bitcast.4, s32[1,30]{1,0:T(1,128)} %av_ref.1, bf16[4,256,1024]{2,1,0:T(8,128)(2,1)} %constant.8.clone.high_hbm, bf16[4,256,1024]{2,1,0:T(8,128)(2,1)} %constant.9.clone.low_hbm, bf16[2,512,384]{2,1,0:T(8,128)(2,1)} %constant.10.clone.place_hbm), custom_call_target="tpu_custom_call" | custom-call | tf_op jit(solution)/shard_map/stack/pallas_call | solution.py:311
  52.5 6.7 %lags.1 = bf16[9,64,2048]{2,1,0:T(8,128)(2,1)} custom-call(bf16[3,32,3,16,128]{4,3,2,1,0:T(8,128)(2,1)} %stack.1.s_ref, bf16[1024,2048]{1,0:T(8,128)(2,1)} %constant.11.clone.t_ref), custom_call_target="tpu_custom_call" | custom-call | tf_op jit(solution)/shard_map/lags/pallas_call | solution.py:364

commit v3 on v2

v3 whole, which is shorter than its diff:
```python
import functools
import math

import jax
import jax.numpy as jnp
import ml_dtypes
import numpy as np
from jax import lax
from jax.experimental import pallas as pl
from jax.experimental.pallas import tpu as pltpu
from jax.sharding import PartitionSpec as P

MESH = pl.DeviceIdType.MESH
F32 = jnp.float32
BF16 = jnp.bfloat16
NFFT = 4096
FREQS = 512
LAG = 1024
SEGS = 30
ROWS = 90
RESIDUES = ((1, 7), (2, 6), (3, 5), (8, 4))
HALF = math.sqrt(0.5)
HALVES = 1
OTHERS = sorted(
    ((dx, dy, dc) for dx in range(4) for dy in range(4) for dc in range(2) if dx or dy or dc),
    key=lambda d: (-min(d[0], 4 - d[0]) - min(d[1], 4 - d[1]), (5 * d[0] + 3 * d[1] + d[2]) % 7),
)
SCHEDULE = (
    ["F010", "F110", "F210", "A01", "F021", "A11", "F121", "A21", "F221"]
    + ["A02", "F032", "F042", "A12", "F132", "F142", "A22", "F232", "F242"]
    + ["A03", "A04", "C0", "S00", "S01", "S02", "S03"]
    + ["A13", "A14", "C1", "S10", "S11", "S12", "S13"]
    + ["A23", "A24", "C2", "S20", "S21", "S22", "S23"]
)
NT = (((1,), (1,)), ((), ()))


def bin_of(p, f):
    return 16 * p + 8 * (f % 2) + np.array(RESIDUES)[f // 4, f // 2 % 2]


def forward_table():
    table = np.zeros((4, 32, 2, 2, 2, 2, 512))
    n = np.arange(512)
    for g in range(4):
        for which in range(2):
            for odd in range(2):
                k = 16 * np.arange(32) + 8 * odd + RESIDUES[g][which]
                angle = (k[:, None] * n[None, :] % NFFT) * (2 * np.pi / NFFT)
                cos, sin = np.cos(angle), np.sin(angle)
                if g == 3:
                    table[g, :, which, odd, 0, which] = cos
                    table[g, :, which, odd, 1, which] = -sin
                else:
                    sign = 1 - 2 * which
                    table[g, :, which, odd, 0, 0] = cos
                    table[g, :, which, odd, 0, 1] = sign * sin
                    table[g, :, which, odd, 1, 0] = -sin
                    table[g, :, which, odd, 1, 1] = sign * cos
    table = table.reshape(4, 256, 1024)
    high = table.astype(ml_dtypes.bfloat16)
    low = (table - high.astype(np.float64)).astype(ml_dtypes.bfloat16)
    return high.reshape(1024, 1024), low.reshape(1024, 1024)


def inverse_table():
    p, f = np.meshgrid(np.arange(32), np.arange(16), indexing="ij")
    k = bin_of(p, f).reshape(-1)
    tau = np.arange(2 * LAG) - LAG
    angle = (k[:, None] * tau[None, :] % NFFT) * (2 * np.pi / NFFT)
    table = np.concatenate([np.cos(angle), -np.sin(angle)], axis=0) * (2.0 / NFFT)
    return table.astype(ml_dtypes.bfloat16)


def place_table():
    plain = np.zeros((2, 2, 128, 4, 128))
    turned = np.zeros((2, 2, 128, 4, 128))
    for seg in range(2):
        for s in range(SEGS):
            for c in range(3):
                for part in range(2):
                    plain[seg, part, 3 * s + c, c, 64 * part + 30 * seg + s] = 1
                turned[seg, 1, 3 * s + c, c, 30 * seg + s] = 1
                turned[seg, 0, 3 * s + c, c, 64 + 30 * seg + s] = -1
    both = np.concatenate([plain.reshape(512, 512), turned.reshape(512, 512)], axis=1)
    return both.astype(ml_dtypes.bfloat16)


def all_tables(inverse):
    return np.concatenate([*forward_table(), inverse[:, :LAG], inverse[:, LAG:], place_table()], axis=0)


def place():
    blk, seg = lax.axis_index("blk"), lax.axis_index("seg")
    z, rest = blk // 16, blk % 16
    return z, rest // 4, seg * 2 + rest // 2 % 2, rest % 2, seg


def device(z, x, y, core):
    return (z * 16 + x * 4 + y % 2 * 2 + core, y // 2)


def lag_rows(blocks):
    turned = [block.T for block in blocks]
    return jnp.concatenate([jnp.concatenate([one[:64], one[64:]], axis=1) for one in turned], axis=0)


def spread(av):
    column = lax.broadcasted_iota(jnp.int32, (SEGS, 128), 1)
    row = lax.broadcasted_iota(jnp.int32, (SEGS, 128), 0)
    pick = ((column >= 3 * row) & (column < 3 * row + 3)).astype(F32)
    return jnp.dot(jnp.broadcast_to(av, (8, SEGS)), pick, preferred_element_type=F32)


def split_rows(w_ref, g, half, value):
    high = value.astype(BF16)
    low = (value - high.astype(F32)).astype(BF16)
    columns = pl.ds(512 * half, 512)
    w_ref[g, pl.ds(0, ROWS), columns] = high
    w_ref[g, pl.ds(128, ROWS), columns] = low


def stack_kernel(
    x_hbm, av_ref, table_hbm, last_ref, lags,
    x_ref, table_ref, stacks,
    w, xs, white, rin, turn, gathered, left, stage, send, counts,
    load_sem, line_sem, core_sem, count_sem, in_sem, ring_send, ring_recv, out_sem, own_sem,
):
    z, x, y, core, seg = place()
    slot = (x * 4 + y % 2 * 2 + core) * 2 + seg
    others = [((x + dx) % 4, (y + dy) % 4, (core + dc) % 2) for dx, dy, dc in OTHERS]
    barrier = pltpu.get_barrier_semaphore()

    lines = [((x + n) % 4, y, core) for n in range(1, 4)]
    near = [device(z, *at) for at in lines]
    near += [device(z, x, (y + n) % 4, core) for n in range(1, 4)]
    near += [device(z, x, y, 1 - core)]
    near += [device((z + n) % 8, x, y, core) for n in (1, 2, 6, 7)]
    for other in near:
        pl.semaphore_signal(barrier, inc=1, device_id=other, device_id_type=MESH)

    parts = [pl.ds(first, rows) for first, rows in ((0, 1024), (1024, 1024), (4096, 512), (2048, 2048))]
    loads = [pltpu.make_async_copy(x_hbm, x_ref, load_sem.at[4])]
    loads += [
        pltpu.make_async_copy(table_hbm.at[rows], table_ref.at[rows], load_sem.at[n]) for n, rows in enumerate(parts)
    ]
    for load in loads:
        load.start()

    own = spread(av_ref[...].astype(F32))
    counts[0] = own
    for g in range(4):
        for start in (80, 208):
            w[g, pl.ds(start, 48), :] = jnp.zeros((48, 1024), BF16)
    loads[0].wait()
    part = [x_ref[:, 0, pl.ds(512 * n, 512)] for n in range(5)]
    part.append(jnp.concatenate([x_ref[:, 0, pl.ds(2560, 440)], jnp.zeros((ROWS, 72), F32)], axis=1))
    d04 = part[0] - part[4]
    d13, s13 = part[1] - part[3], part[1] + part[3]
    split_rows(w, 0, 0, d04 + (d13 - part[5]) * HALF)
    split_rows(w, 0, 1, (part[5] - s13) * HALF - part[2])
    split_rows(w, 1, 0, part[0] + part[4] - part[2])
    split_rows(w, 1, 1, part[3] - part[1] - part[5])
    split_rows(w, 2, 0, d04 + (part[5] - d13) * HALF)
    split_rows(w, 2, 1, (part[5] - s13) * HALF + part[2])
    even, odd = part[0] + part[2] + part[4], s13 + part[5]
    split_rows(w, 3, 0, even + odd)
    split_rows(w, 3, 1, even - odd)

    pl.semaphore_wait(barrier, 11)
    for at in lines:
        pl.semaphore_signal(line_sem, inc=1, device_id=device(z, *at), device_id_type=MESH)
    count_copy = pltpu.make_async_remote_copy(
        src_ref=counts.at[0], dst_ref=counts.at[1], send_sem=count_sem.at[0], recv_sem=count_sem.at[1],
        device_id=device(z, x, (y + 2) % 4, core), device_id_type=MESH,
    )
    count_copy.start()

    power = jnp.zeros((32, 8, 128), F32)
    loads[1].wait()
    loads[2].wait()
    for g in range(4):
        if g == 2:
            pl.semaphore_wait(line_sem, 3)
            pl.semaphore_signal(core_sem, inc=1, device_id=device(z, x, y, 1 - core), device_id_type=MESH)
        high = lax.dot_general(table_ref[256 * g : 256 * (g + 1)], w[g], NT, preferred_element_type=F32)
        low = lax.dot_general(table_ref[1024 + 256 * g : 1280 + 256 * g], w[g], NT, preferred_element_type=F32)
        both = high + low
        value = (both[:, :128] + both[:, 128:]).reshape(32, 8, 128)
        xs[:, pl.ds(8 * g, 8), :] = value
        power = power + value * value
    power = jnp.sum(power.reshape(16, 16, 128), axis=1)
    triple = power + pltpu.roll(power, 127, 1) + pltpu.roll(power, 126, 1)
    phase = lax.broadcasted_iota(jnp.int32, (16, 128), 1) % 3
    total = jnp.where(phase == 0, triple, jnp.where(phase == 1, pltpu.roll(triple, 1, 1), pltpu.roll(triple, 2, 1)))
    amplitude = jnp.sqrt(total * (1.0 / 96) + 1e-06)
    count_copy.wait()
    count = (jnp.sum(own, axis=1, keepdims=True) + jnp.sum(counts[1], axis=1, keepdims=True)) * (1.0 / 3)
    weight = own / jnp.sqrt(jnp.round(count))
    factor = weight[0:1] / amplitude
    white[...] = (xs[...].reshape(16, 64, 128) * factor[:, None, :]).reshape(32, 32, 128).astype(BF16)

    pl.semaphore_wait(core_sem, 1)

    for px, py, pc in others:
        target = (px * 4 + py % 2 * 2 + pc) * 2 + py // 2
        pltpu.make_async_remote_copy(
            src_ref=white.at[target], dst_ref=rin.at[slot], send_sem=in_sem.at[0], recv_sem=in_sem.at[1],
            device_id=device(z, px, py, pc), device_id_type=MESH,
        ).start()
    pltpu.make_async_copy(rin.at[pl.ds(0, 31)], rin.at[pl.ds(0, 31)], in_sem.at[1]).wait()
    rin[slot] = white[slot]

    def swap(source, carry):
        start = source % 2 * 512 + source // 2
        turn[pl.ds(start, 32, stride=16), :] = rin[source].astype(F32)
        return carry

    lax.fori_loop(0, 32, swap, 0)
    loads[3].wait()
    pieces = turn[...].reshape(2, 16, 2, 16, 128)
    rows = jnp.concatenate(
        [pieces[s, :, part].reshape(256, 128).astype(BF16) for s in range(2) for part in range(2)], axis=1
    )
    plain = jnp.dot(rows, table_ref[4096:, :384], preferred_element_type=F32).astype(BF16)
    turned = jnp.dot(rows, table_ref[4096:, 512:896], preferred_element_type=F32).astype(BF16)
    for c in range(3):
        one = plain[:, 128 * c : 128 * (c + 1)].reshape(16, 16, 128)
        gathered[c, z] = one
        left[:, pl.ds(16 * c, 16), :] = one
        left[:, pl.ds(48 + 16 * c, 16), :] = turned[:, 128 * c : 128 * (c + 1)].reshape(16, 16, 128)

    def moves(u, reach, come):
        size = 16 // HALVES
        signs = (1, -1) if reach < 4 else (1 - 2 * core,)
        for way, sign in enumerate(signs):
            piece = gathered.at[u // HALVES, (z + 8 - sign * come) % 8, pl.ds(u % HALVES * size, size)]
            yield pltpu.make_async_remote_copy(
                src_ref=piece, dst_ref=piece,
                send_sem=ring_send.at[u, reach - 1, way], recv_sem=ring_recv.at[u, reach - 1, way],
                device_id=device((z + 8 + sign * (reach - come)) % 8, x, y, core), device_id_type=MESH,
            )

    def forward(u, reach, come):
        for copy in moves(u, reach, come):
            copy.start()

    def arrive(u, reach):
        for copy in moves(u, reach, 0):
            copy.wait_recv()

    lane = lax.broadcasted_iota(jnp.int32, (16, 128), 1) < 64

    def cross(b):
        def four_bins(step, carry):
            for f in [4 * step + n for n in range(4)]:
                right = gathered[b, :, f].reshape(128, 128)
                product = lax.dot_general(left[f], right, NT, preferred_element_type=F32)
                for a in range(3):
                    re = product[16 * a : 16 * (a + 1)]
                    im = product[48 + 16 * a : 48 + 16 * (a + 1)]
                    mixed = pltpu.roll(jnp.where(lane, im, re), 64, 1)
                    stage[pl.ds(512 * a + f, 16, stride=16), :] = jnp.where(lane, re, mixed)
                    stage[pl.ds(512 * a + 256 + f, 16, stride=16), :] = jnp.where(lane, mixed, im)
            return carry

        lax.fori_loop(0, 4, four_bins, 0)
        send[b] = jnp.stack([stage[pl.ds(512 * a, 512), :].reshape(2, 16, 16, 128).astype(BF16) for a in range(3)], axis=2)

    def keep(b):
        target = stacks.at[b, slot] if b < 2 else last_ref.at[slot]
        return pltpu.make_async_copy(send.at[b, seg, slot // 2], target, own_sem.at[b])

    def ship(b, quarter):
        for px, py, pc in others[8 * quarter : 8 * quarter + 8]:
            pltpu.make_async_remote_copy(
                src_ref=send.at[b, py // 2, px * 4 + py % 2 * 2 + pc], dst_ref=stacks.at[b, slot] if b < 2 else last_ref.at[slot],
                send_sem=out_sem.at[b, 0], recv_sem=out_sem.at[b, 1],
                device_id=device(z, px, py, pc), device_id_type=MESH,
            ).start()
        if quarter == 3:
            keep(b).start()

    steps = {"F": forward, "A": arrive, "C": cross, "S": ship}
    for step in SCHEDULE:
        steps[step[0]](*(int(digit) for digit in step[1:]))

    loads[4].wait()
    for b in range(2):
        keep(b).wait()
        whole = stacks.at[b, pl.ds(0, 31)]
        pltpu.make_async_copy(whole, whole, out_sem.at[b, 1]).wait()
        rows = lag_rows([stacks[b, :, a].reshape(512, 128) for a in range(3)])
        for n in range(4):
            half = table_ref[2048 + 1024 * (n // 2) : 3072 + 1024 * (n // 2), 512 * (n % 2) : 512 * (n % 2 + 1)]
            lagged = jnp.dot(rows, half, preferred_element_type=F32)
            lags[b, :, :, pl.ds(512 * n, 512)] = lagged.astype(BF16).reshape(3, 64, 512)

    pltpu.make_async_copy(white.at[pl.ds(0, 31)], white.at[pl.ds(0, 31)], in_sem.at[0]).wait()
    for u in range(3 * HALVES):
        for reach in range(1, 5):
            for copy in moves(u, reach, 0):
                copy.wait_send()
    keep(2).wait()
    whole = last_ref.at[pl.ds(0, 31)]
    pltpu.make_async_copy(whole, whole, out_sem.at[2, 1]).wait()
    for b in range(3):
        pltpu.make_async_copy(whole, whole, out_sem.at[b, 0]).wait()


def in_hbm(array):
    return pltpu.with_memory_space_constraint(array, pltpu.HBM)


def stacked(records, availability, tables):
    vmem, hbm = pl.BlockSpec(memory_space=pltpu.VMEM), pl.BlockSpec(memory_space=pl.ANY)
    return pl.pallas_call(
        stack_kernel,
        name="stack",
        out_shape=(
            pltpu.VMEM((32, 3, 16, 128), BF16),
            pltpu.VMEM((2, 3, 64, 2 * LAG), BF16),
        ),
        in_specs=[hbm, vmem, hbm],
        out_specs=(vmem, vmem),
        scratch_shapes=[
            pltpu.VMEM(records.shape, F32),
            pltpu.VMEM(tables.shape, BF16),
            pltpu.VMEM((2, 32, 3, 16, 128), BF16),
            pltpu.VMEM((4, 256, 1024), BF16),
            pltpu.VMEM((32, 32, 128), F32),
            pltpu.VMEM((32, 32, 128), BF16),
            pltpu.VMEM((32, 32, 128), BF16),
            pltpu.VMEM((1024, 128), F32),
            pltpu.VMEM((3, 8, 16, 16, 128), BF16),
            pltpu.VMEM((16, 96, 128), BF16),
            pltpu.VMEM((1536, 128), F32),
            pltpu.VMEM((3, 2, 16, 3, 16, 128), BF16),
            pltpu.VMEM((2, 8, 128), F32),
            pltpu.SemaphoreType.DMA((5,)),
            pltpu.SemaphoreType.REGULAR,
            pltpu.SemaphoreType.REGULAR,
            pltpu.SemaphoreType.DMA((2,)),
            pltpu.SemaphoreType.DMA((2,)),
            pltpu.SemaphoreType.DMA((3 * HALVES, 4, 2)),
            pltpu.SemaphoreType.DMA((3 * HALVES, 4, 2)),
            pltpu.SemaphoreType.DMA((3, 2)),
            pltpu.SemaphoreType.DMA((3,)),
        ],
        compiler_params=pltpu.CompilerParams(
            collective_id=0, has_side_effects=True, vmem_limit_bytes=40 << 20
        ),
    )(in_hbm(records), in_hbm(availability), in_hbm(tables))


def lag_kernel(last_ref, part_ref, table_ref, out_hbm, lags, part_sem, out_sem):
    copies = [
        pltpu.make_async_copy(part_ref.at[b, a], out_hbm.at[3 * a + b], part_sem.at[b, a])
        for b in range(2)
        for a in range(3)
    ]
    for copy in copies:
        copy.start()
    rows = lag_rows([last_ref[:, a].reshape(512, 128) for a in range(3)])
    for n in range(4):
        column = pl.ds(512 * n, 512)
        lagged = jnp.dot(rows, table_ref[:, column], preferred_element_type=F32)
        lags[:, :, column] = lagged.astype(BF16).reshape(3, 64, 512)
        for a in range(3):
            copies.append(
                pltpu.make_async_copy(
                    lags.at[a, :, column], out_hbm.at[3 * a + 2, :, column], out_sem.at[n, a]
                )
            )
            copies[-1].start()
    for copy in copies:
        copy.wait()


def to_lags(last, part, table):
    vmem = pl.BlockSpec(memory_space=pltpu.VMEM)
    return pl.pallas_call(
        lag_kernel,
        name="lags",
        out_shape=jax.ShapeDtypeStruct((9, 64, 2 * LAG), BF16),
        in_specs=[vmem] * 3,
        out_specs=pl.BlockSpec(memory_space=pl.ANY),
        scratch_shapes=[
            pltpu.VMEM((3, 64, 2 * LAG), BF16),
            pltpu.SemaphoreType.DMA((2, 3)),
            pltpu.SemaphoreType.DMA((4, 3)),
        ],
        compiler_params=pltpu.CompilerParams(vmem_limit_bytes=40 << 20),
    )(*(pltpu.with_memory_space_constraint(array, pltpu.VMEM) for array in (last, part, table)))


def body(records, availability):
    samples = records.shape[-1]
    inverse = inverse_table()
    last, part = stacked(records.reshape(ROWS, 1, samples), availability, jnp.asarray(all_tables(inverse)))
    lagged = to_lags(last, part, jnp.asarray(inverse))
    return jnp.transpose(lagged, (1, 0, 2))[None]


def solution(mesh):
    placed = (P("blk", "seg", None, None), P("blk", "seg"))
    return jax.shard_map(
        body, mesh=mesh, in_specs=placed, out_specs=P("blk", "seg", None, None), check_vma=False
    )
```

time: 59.3 us -> 53.5 us (0.902)
  Pallas kernels: 59.2 us -> 53.4 us
    pallas_call x2, Pallas kernels: 59.2 us -> 53.4 us  [the longest x1 51.5 us: stacked(): pl.pallas_call(stack_kernel, name='stack', out_shape=(pltpu.VMEM((32, 3,...]
where the time goes in v3:
time: 53.5 us; the launch traced here: 53.4 us
  Pallas kernels  53.4 us (100%)
    pallas_call x1, Pallas kernels, stacked(): pl.pallas_call(stack_kernel, name='stack', out_shape=(pltpu.VMEM((32, 3,...  51.5 us
    pallas_call x1, Pallas kernels, to_lags(): pl.pallas_call(lag_kernel, name='lags', out_shape=jax.ShapeDtypeStruct((9...  1.85 us

profile of v3, /device:TPU:1, one launch (start us, length us, event | category | flops | bytes accessed | tf_op | source)
XLA Modules:
  0.0 53.4 jit_solution(1578652198862386846)
XLA Ops:
  0.0 0.0 copy-start
  0.0 51.5 %stack.1 = (bf16[32,3,16,128]{3,2,1,0:T(8,128)(2,1)S(1)}, bf16[2,3,64,2048]{3,2,1,0:T(8,128)(2,1)S(1)}) custom-call(f32[90,1,3000]{2,1,0:T(1,128)} %bitcast.4, s32[1,30]{1,0:T(1,128)} %av_ref.1, bf16[4608,1024]{1,0:T(8,128)(2,1)} %constant.4.clone.table_hbm), custom_call_target="tpu_custom_call" | custom-call | tf_op jit(solution)/shard_map/stack/pallas_call | solution.py:317
  51.6 0.0 copy-done
  51.6 1.8 %lags.1 = bf16[9,64,2048]{2,1,0:T(8,128)(2,1)} custom-call(bf16[32,3,16,128]{3,2,1,0:T(8,128)(2,1)S(1)} %get-tuple-element.7.last_ref, bf16[2,3,64,2048]{3,2,1,0:T(8,128)(2,1)S(1)} %get-tuple-element.8.part_ref, bf16[1024,2048]{1,0:T(8,128)(2,1)S(1)} %copy-done), custom_call_target="tpu_custom_call" | custom-call | tf_op jit(solution)/shard_map/lags/pallas_call | solution.py:382
Async XLA Ops:
  0.0 51.6 %copy-start = (bf16[1024,2048]{1,0:T(8,128)(2,1)S(1)}, bf16[1024,2048]{1,0:T(8,128)(2,1)}, u32[]{:S(2)}) copy-start(bf16[1024,2048]{1,0:T(8,128)(2,1)} %constant.5.clone.table_ref) | copy-start | bytes 12582916

commit v4 on v3

--- a/solution.py
+++ b/solution.py
@@ -26,9 +26,9 @@
     key=lambda d: (-min(d[0], 4 - d[0]) - min(d[1], 4 - d[1]), (5 * d[0] + 3 * d[1] + d[2]) % 7),
 )
 SCHEDULE = (
-    ["F010", "F110", "F210", "A01", "F021", "A11", "F121", "A21", "F221"]
-    + ["A02", "F032", "F042", "A12", "F132", "F142", "A22", "F232", "F242"]
-    + ["A03", "A04", "C0", "S00", "S01", "S02", "S03"]
+    ["F010", "F110", "L", "A01", "F021", "F210", "A11", "F121", "A02", "F032", "F042"]
+    + ["A21", "F221", "A12", "F132", "F142", "A03", "A04", "C0"]
+    + ["S00", "S01", "A22", "F232", "F242", "S02", "S03"]
     + ["A13", "A14", "C1", "S10", "S11", "S12", "S13"]
     + ["A23", "A24", "C2", "S20", "S21", "S22", "S23"]
 )
@@ -121,32 +121,33 @@
 
 
 def stack_kernel(
-    x_hbm, av_ref, table_hbm, last_ref, lags,
-    x_ref, table_ref, stacks,
+    x_hbm, av_hbm, table_hbm, last_ref, lags,
+    x_ref, av_ref, table_ref, stacks,
     w, xs, white, rin, turn, gathered, left, stage, send, counts,
     load_sem, line_sem, core_sem, count_sem, in_sem, ring_send, ring_recv, out_sem, own_sem,
 ):
     z, x, y, core, seg = place()
     slot = (x * 4 + y % 2 * 2 + core) * 2 + seg
     others = [((x + dx) % 4, (y + dy) % 4, (core + dc) % 2) for dx, dy, dc in OTHERS]
-    barrier = pltpu.get_barrier_semaphore()
-
-    lines = [((x + n) % 4, y, core) for n in range(1, 4)]
-    near = [device(z, *at) for at in lines]
-    near += [device(z, x, (y + n) % 4, core) for n in range(1, 4)]
-    near += [device(z, x, y, 1 - core)]
-    near += [device((z + n) % 8, x, y, core) for n in (1, 2, 6, 7)]
-    for other in near:
-        pl.semaphore_signal(barrier, inc=1, device_id=other, device_id_type=MESH)
-
     parts = [pl.ds(first, rows) for first, rows in ((0, 1024), (1024, 1024), (4096, 512), (2048, 2048))]
-    loads = [pltpu.make_async_copy(x_hbm, x_ref, load_sem.at[4])]
+    loads = [pltpu.make_async_copy(x_hbm, x_ref, load_sem.at[4]), pltpu.make_async_copy(av_hbm, av_ref, load_sem.at[5])]
     loads += [
         pltpu.make_async_copy(table_hbm.at[rows], table_ref.at[rows], load_sem.at[n]) for n, rows in enumerate(parts)
     ]
     for load in loads:
         load.start()
 
+    barrier = pltpu.get_barrier_semaphore()
+
+    lines = [((x + n) % 4, y, core) for n in range(1, 4)]
+    near = [device(z, x, (y + n) % 4, core) for n in (2, 1, 3)]
+    near += [device(z, *at) for at in lines]
+    near += [device(z, x, y, 1 - core)]
+    near += [device((z + n) % 8, x, y, core) for n in (1, 2, 6, 7)]
+    for other in near:
+        pl.semaphore_signal(barrier, inc=1, device_id=other, device_id_type=MESH)
+
+    loads[1].wait()
     own = spread(av_ref[...].astype(F32))
     counts[0] = own
     for g in range(4):
@@ -168,17 +169,17 @@
     split_rows(w, 3, 1, even - odd)
 
     pl.semaphore_wait(barrier, 11)
-    for at in lines:
-        pl.semaphore_signal(line_sem, inc=1, device_id=device(z, *at), device_id_type=MESH)
     count_copy = pltpu.make_async_remote_copy(
         src_ref=counts.at[0], dst_ref=counts.at[1], send_sem=count_sem.at[0], recv_sem=count_sem.at[1],
         device_id=device(z, x, (y + 2) % 4, core), device_id_type=MESH,
     )
     count_copy.start()
+    for at in lines:
+        pl.semaphore_signal(line_sem, inc=1, device_id=device(z, *at), device_id_type=MESH)
 
     power = jnp.zeros((32, 8, 128), F32)
-    loads[1].wait()
     loads[2].wait()
+    loads[3].wait()
     for g in range(4):
         if g == 2:
             pl.semaphore_wait(line_sem, 3)
@@ -217,18 +218,14 @@
         return carry
 
     lax.fori_loop(0, 32, swap, 0)
-    loads[3].wait()
+    loads[4].wait()
     pieces = turn[...].reshape(2, 16, 2, 16, 128)
     rows = jnp.concatenate(
         [pieces[s, :, part].reshape(256, 128).astype(BF16) for s in range(2) for part in range(2)], axis=1
     )
     plain = jnp.dot(rows, table_ref[4096:, :384], preferred_element_type=F32).astype(BF16)
-    turned = jnp.dot(rows, table_ref[4096:, 512:896], preferred_element_type=F32).astype(BF16)
     for c in range(3):
-        one = plain[:, 128 * c : 128 * (c + 1)].reshape(16, 16, 128)
-        gathered[c, z] = one
-        left[:, pl.ds(16 * c, 16), :] = one
-        left[:, pl.ds(48 + 16 * c, 16), :] = turned[:, 128 * c : 128 * (c + 1)].reshape(16, 16, 128)
+        gathered[c, z] = plain[:, 128 * c : 128 * (c + 1)].reshape(16, 16, 128)
 
     def moves(u, reach, come):
         size = 16 // HALVES
@@ -249,22 +246,24 @@
         for copy in moves(u, reach, 0):
             copy.wait_recv()
 
+    def own_side():
+        turned = jnp.dot(rows, table_ref[4096:, 512:896], preferred_element_type=F32).astype(BF16)
+        for c in range(3):
+            left[:, pl.ds(16 * c, 16), :] = plain[:, 128 * c : 128 * (c + 1)].reshape(16, 16, 128)
+            left[:, pl.ds(48 + 16 * c, 16), :] = turned[:, 128 * c : 128 * (c + 1)].reshape(16, 16, 128)
+
     lane = lax.broadcasted_iota(jnp.int32, (16, 128), 1) < 64
 
     def cross(b):
-        def four_bins(step, carry):
-            for f in [4 * step + n for n in range(4)]:
-                right = gathered[b, :, f].reshape(128, 128)
-                product = lax.dot_general(left[f], right, NT, preferred_element_type=F32)
-                for a in range(3):
-                    re = product[16 * a : 16 * (a + 1)]
-                    im = product[48 + 16 * a : 48 + 16 * (a + 1)]
-                    mixed = pltpu.roll(jnp.where(lane, im, re), 64, 1)
-                    stage[pl.ds(512 * a + f, 16, stride=16), :] = jnp.where(lane, re, mixed)
-                    stage[pl.ds(512 * a + 256 + f, 16, stride=16), :] = jnp.where(lane, mixed, im)
-            return carry
-
-        lax.fori_loop(0, 4, four_bins, 0)
+        for f in range(16):
+            right = gathered[b, :, f].reshape(128, 128)
+            product = lax.dot_general(left[f], right, NT, preferred_element_type=F32)
+            for a in range(3):
+                re = product[16 * a : 16 * (a + 1)]
+                im = product[48 + 16 * a : 48 + 16 * (a + 1)]
+                mixed = pltpu.roll(jnp.where(lane, im, re), 64, 1)
+                stage[pl.ds(512 * a + f, 16, stride=16), :] = jnp.where(lane, re, mixed)
+                stage[pl.ds(512 * a + 256 + f, 16, stride=16), :] = jnp.where(lane, mixed, im)
         send[b] = jnp.stack([stage[pl.ds(512 * a, 512), :].reshape(2, 16, 16, 128).astype(BF16) for a in range(3)], axis=2)
 
     def keep(b):
@@ -281,11 +280,11 @@
         if quarter == 3:
             keep(b).start()
 
-    steps = {"F": forward, "A": arrive, "C": cross, "S": ship}
+    steps = {"F": forward, "A": arrive, "L": own_side, "C": cross, "S": ship}
     for step in SCHEDULE:
         steps[step[0]](*(int(digit) for digit in step[1:]))
 
-    loads[4].wait()
+    loads[5].wait()
     for b in range(2):
         keep(b).wait()
         whole = stacks.at[b, pl.ds(0, 31)]
@@ -321,10 +320,11 @@
             pltpu.VMEM((32, 3, 16, 128), BF16),
             pltpu.VMEM((2, 3, 64, 2 * LAG), BF16),
         ),
-        in_specs=[hbm, vmem, hbm],
+        in_specs=[hbm, hbm, hbm],
         out_specs=(vmem, vmem),
         scratch_shapes=[
             pltpu.VMEM(records.shape, F32),
+            pltpu.VMEM(availability.shape, jnp.int32),
             pltpu.VMEM(tables.shape, BF16),
             pltpu.VMEM((2, 32, 3, 16, 128), BF16),
             pltpu.VMEM((4, 256, 1024), BF16),
@@ -337,7 +337,7 @@
             pltpu.VMEM((1536, 128), F32),
             pltpu.VMEM((3, 2, 16, 3, 16, 128), BF16),
             pltpu.VMEM((2, 8, 128), F32),
-            pltpu.SemaphoreType.DMA((5,)),
+            pltpu.SemaphoreType.DMA((6,)),
             pltpu.SemaphoreType.REGULAR,
             pltpu.SemaphoreType.REGULAR,
             pltpu.SemaphoreType.DMA((2,)),

time: 53.5 us -> 50.8 us (0.950)
  Pallas kernels: 53.4 us -> 50.7 us
    pallas_call x1, Pallas kernels: 51.5 us -> 48.8 us  [stacked(): pl.pallas_call(stack_kernel, name='stack', out_shape=(pltpu.VMEM((32, 3,...]
where the time goes in v4:
time: 50.8 us; the launch traced here: 50.7 us
  Pallas kernels  50.7 us (100%)
    pallas_call x1, Pallas kernels, stacked(): pl.pallas_call(stack_kernel, name='stack', out_shape=(pltpu.VMEM((32, 3,...  48.8 us
    pallas_call x1, Pallas kernels, to_lags(): pl.pallas_call(lag_kernel, name='lags', out_shape=jax.ShapeDtypeStruct((9...  1.85 us

profile of v4, /device:TPU:1, one launch (start us, length us, event | category | flops | bytes accessed | tf_op | source)
XLA Modules:
  0.0 50.7 jit_solution(17572327968387243306)
XLA Ops:
  0.0 0.0 copy-start
  0.0 48.8 %stack.1 = (bf16[32,3,16,128]{3,2,1,0:T(8,128)(2,1)S(1)}, bf16[2,3,64,2048]{3,2,1,0:T(8,128)(2,1)S(1)}) custom-call(f32[90,1,3000]{2,1,0:T(1,128)} %bitcast.4, s32[1,30]{1,0:T(1,128)} %av_hbm.1, bf16[4608,1024]{1,0:T(8,128)(2,1)} %constant.4.clone.table_hbm), custom_call_target="tpu_custom_call" | custom-call | tf_op jit(solution)/shard_map/stack/pallas_call | solution.py:316
  48.8 0.0 copy-done
  48.9 1.8 %lags.1 = bf16[9,64,2048]{2,1,0:T(8,128)(2,1)} custom-call(bf16[32,3,16,128]{3,2,1,0:T(8,128)(2,1)S(1)} %get-tuple-element.7.last_ref, bf16[2,3,64,2048]{3,2,1,0:T(8,128)(2,1)S(1)} %get-tuple-element.8.part_ref, bf16[1024,2048]{1,0:T(8,128)(2,1)S(1)} %copy-done), custom_call_target="tpu_custom_call" | custom-call | tf_op jit(solution)/shard_map/lags/pallas_call | solution.py:382
Async XLA Ops:
  0.0 48.8 %copy-start = (bf16[1024,2048]{1,0:T(8,128)(2,1)S(1)}, bf16[1024,2048]{1,0:T(8,128)(2,1)}, u32[]{:S(2)}) copy-start(bf16[1024,2048]{1,0:T(8,128)(2,1)} %constant.5.clone.table_ref) | copy-start | bytes 12582916

commit v5 on v4

--- a/solution.py
+++ b/solution.py
@@ -17,20 +17,20 @@
 FREQS = 512
 LAG = 1024
 SEGS = 30
-ROWS = 90
+ROWS = 96
 RESIDUES = ((1, 7), (2, 6), (3, 5), (8, 4))
 HALF = math.sqrt(0.5)
-HALVES = 1
+UNITS = ((0, 0, 8), (0, 8, 8), (1, 0, 16), (2, 0, 16))
 OTHERS = sorted(
     ((dx, dy, dc) for dx in range(4) for dy in range(4) for dc in range(2) if dx or dy or dc),
     key=lambda d: (-min(d[0], 4 - d[0]) - min(d[1], 4 - d[1]), (5 * d[0] + 3 * d[1] + d[2]) % 7),
 )
 SCHEDULE = (
-    ["F010", "F110", "L", "A01", "F021", "F210", "A11", "F121", "A02", "F032", "F042"]
-    + ["A21", "F221", "A12", "F132", "F142", "A03", "A04", "C0"]
-    + ["S00", "S01", "A22", "F232", "F242", "S02", "S03"]
-    + ["A13", "A14", "C1", "S10", "S11", "S12", "S13"]
-    + ["A23", "A24", "C2", "S20", "S21", "S22", "S23"]
+    ["P0", "F010", "P1", "F110", "F210", "L", "A01", "F021", "A11", "F121", "F310", "A21", "F221"]
+    + ["A02", "F032", "F042", "A12", "F132", "F142", "A31", "F321", "A22", "F232", "F242"]
+    + ["A03", "A13", "A04", "A14", "C0", "S00", "S01", "A32", "F332", "F342", "S02", "S03"]
+    + ["A23", "A24", "C1", "S10", "S11", "S12", "S13"]
+    + ["A33", "A34", "C2", "S20", "S21", "S22", "S23"]
 )
 NT = (((1,), (1,)), ((), ()))
 
@@ -130,7 +130,7 @@
     slot = (x * 4 + y % 2 * 2 + core) * 2 + seg
     others = [((x + dx) % 4, (y + dy) % 4, (core + dc) % 2) for dx, dy, dc in OTHERS]
     parts = [pl.ds(first, rows) for first, rows in ((0, 1024), (1024, 1024), (4096, 512), (2048, 2048))]
-    loads = [pltpu.make_async_copy(x_hbm, x_ref, load_sem.at[4]), pltpu.make_async_copy(av_hbm, av_ref, load_sem.at[5])]
+    loads = [pltpu.make_async_copy(x_hbm, x_ref.at[pl.ds(0, 90)], load_sem.at[4]), pltpu.make_async_copy(av_hbm, av_ref, load_sem.at[5])]
     loads += [
         pltpu.make_async_copy(table_hbm.at[rows], table_ref.at[rows], load_sem.at[n]) for n, rows in enumerate(parts)
     ]
@@ -151,8 +151,9 @@
     own = spread(av_ref[...].astype(F32))
     counts[0] = own
     for g in range(4):
-        for start in (80, 208):
-            w[g, pl.ds(start, 48), :] = jnp.zeros((48, 1024), BF16)
+        for start in (ROWS, 128 + ROWS):
+            w[g, pl.ds(start, 32), :] = jnp.zeros((32, 1024), BF16)
+    x_ref[pl.ds(90, ROWS - 90)] = jnp.zeros((ROWS - 90, 1, x_ref.shape[2]), F32)
     loads[0].wait()
     part = [x_ref[:, 0, pl.ds(512 * n, 512)] for n in range(5)]
     part.append(jnp.concatenate([x_ref[:, 0, pl.ds(2560, 440)], jnp.zeros((ROWS, 72), F32)], axis=1))
@@ -223,15 +224,17 @@
     rows = jnp.concatenate(
         [pieces[s, :, part].reshape(256, 128).astype(BF16) for s in range(2) for part in range(2)], axis=1
     )
-    plain = jnp.dot(rows, table_ref[4096:, :384], preferred_element_type=F32).astype(BF16)
-    for c in range(3):
-        gathered[c, z] = plain[:, 128 * c : 128 * (c + 1)].reshape(16, 16, 128)
+    def own_units(half):
+        plain = jnp.dot(rows[128 * half : 128 * half + 128], table_ref[4096:, :384], preferred_element_type=F32)
+        plain = plain.astype(BF16)
+        for c in range(3):
+            gathered[c, z, pl.ds(8 * half, 8)] = plain[:, 128 * c : 128 * (c + 1)].reshape(8, 16, 128)
 
     def moves(u, reach, come):
-        size = 16 // HALVES
+        c, first, bins = UNITS[u]
         signs = (1, -1) if reach < 4 else (1 - 2 * core,)
         for way, sign in enumerate(signs):
-            piece = gathered.at[u // HALVES, (z + 8 - sign * come) % 8, pl.ds(u % HALVES * size, size)]
+            piece = gathered.at[c, (z + 8 - sign * come) % 8, pl.ds(first, bins)]
             yield pltpu.make_async_remote_copy(
                 src_ref=piece, dst_ref=piece,
                 send_sem=ring_send.at[u, reach - 1, way], recv_sem=ring_recv.at[u, reach - 1, way],
@@ -249,7 +252,7 @@
     def own_side():
         turned = jnp.dot(rows, table_ref[4096:, 512:896], preferred_element_type=F32).astype(BF16)
         for c in range(3):
-            left[:, pl.ds(16 * c, 16), :] = plain[:, 128 * c : 128 * (c + 1)].reshape(16, 16, 128)
+            left[:, pl.ds(16 * c, 16), :] = gathered[c, z]
             left[:, pl.ds(48 + 16 * c, 16), :] = turned[:, 128 * c : 128 * (c + 1)].reshape(16, 16, 128)
 
     lane = lax.broadcasted_iota(jnp.int32, (16, 128), 1) < 64
@@ -280,7 +283,7 @@
         if quarter == 3:
             keep(b).start()
 
-    steps = {"F": forward, "A": arrive, "L": own_side, "C": cross, "S": ship}
+    steps = {"F": forward, "A": arrive, "P": own_units, "L": own_side, "C": cross, "S": ship}
     for step in SCHEDULE:
         steps[step[0]](*(int(digit) for digit in step[1:]))
 
@@ -296,7 +299,7 @@
             lags[b, :, :, pl.ds(512 * n, 512)] = lagged.astype(BF16).reshape(3, 64, 512)
 
     pltpu.make_async_copy(white.at[pl.ds(0, 31)], white.at[pl.ds(0, 31)], in_sem.at[0]).wait()
-    for u in range(3 * HALVES):
+    for u in range(len(UNITS)):
         for reach in range(1, 5):
             for copy in moves(u, reach, 0):
                 copy.wait_send()
@@ -323,7 +326,7 @@
         in_specs=[hbm, hbm, hbm],
         out_specs=(vmem, vmem),
         scratch_shapes=[
-            pltpu.VMEM(records.shape, F32),
+            pltpu.VMEM((ROWS, 1, records.shape[2]), F32),
             pltpu.VMEM(availability.shape, jnp.int32),
             pltpu.VMEM(tables.shape, BF16),
             pltpu.VMEM((2, 32, 3, 16, 128), BF16),
@@ -342,8 +345,8 @@
             pltpu.SemaphoreType.REGULAR,
             pltpu.SemaphoreType.DMA((2,)),
             pltpu.SemaphoreType.DMA((2,)),
-            pltpu.SemaphoreType.DMA((3 * HALVES, 4, 2)),
-            pltpu.SemaphoreType.DMA((3 * HALVES, 4, 2)),
+            pltpu.SemaphoreType.DMA((len(UNITS), 4, 2)),
+            pltpu.SemaphoreType.DMA((len(UNITS), 4, 2)),
             pltpu.SemaphoreType.DMA((3, 2)),
             pltpu.SemaphoreType.DMA((3,)),
         ],
@@ -397,7 +400,7 @@
 def body(records, availability):
     samples = records.shape[-1]
     inverse = inverse_table()
-    last, part = stacked(records.reshape(ROWS, 1, samples), availability, jnp.asarray(all_tables(inverse)))
+    last, part = stacked(records.reshape(90, 1, samples), availability, jnp.asarray(all_tables(inverse)))
     lagged = to_lags(last, part, jnp.asarray(inverse))
     return jnp.transpose(lagged, (1, 0, 2))[None]
 

time: 50.8 us -> 50.8 us (level)
  no operation moved by 1% of the time
where the time goes in v5:
time: 50.8 us
  Pallas kernels  50.7 us (100%)
    pallas_call x1, Pallas kernels, stacked(): pl.pallas_call(stack_kernel, name='stack', out_shape=(pltpu.VMEM((32, 3,...  48.9 us
    pallas_call x1, Pallas kernels, to_lags(): pl.pallas_call(lag_kernel, name='lags', out_shape=jax.ShapeDtypeStruct((9...  1.85 us

profile of v5, /device:TPU:1, one launch (start us, length us, event | category | flops | bytes accessed | tf_op | source)
XLA Modules:
  0.0 50.8 jit_solution(4465331236683586918)
XLA Ops:
  0.0 0.0 copy-start
  0.0 48.9 %stack.1 = (bf16[32,3,16,128]{3,2,1,0:T(8,128)(2,1)S(1)}, bf16[2,3,64,2048]{3,2,1,0:T(8,128)(2,1)S(1)}) custom-call(f32[90,1,3000]{2,1,0:T(1,128)} %bitcast.4, s32[1,30]{1,0:T(1,128)} %av_hbm.1, bf16[4608,1024]{1,0:T(8,128)(2,1)} %constant.4.clone.table_hbm), custom_call_target="tpu_custom_call" | custom-call | tf_op jit(solution)/shard_map/stack/pallas_call | solution.py:319
  48.9 0.0 copy-done
  48.9 1.8 %lags.1 = bf16[9,64,2048]{2,1,0:T(8,128)(2,1)} custom-call(bf16[32,3,16,128]{3,2,1,0:T(8,128)(2,1)S(1)} %get-tuple-element.7.last_ref, bf16[2,3,64,2048]{3,2,1,0:T(8,128)(2,1)S(1)} %get-tuple-element.8.part_ref, bf16[1024,2048]{1,0:T(8,128)(2,1)S(1)} %copy-done), custom_call_target="tpu_custom_call" | custom-call | tf_op jit(solution)/shard_map/lags/pallas_call | solution.py:385
Async XLA Ops:
  0.0 48.9 %copy-start = (bf16[1024,2048]{1,0:T(8,128)(2,1)S(1)}, bf16[1024,2048]{1,0:T(8,128)(2,1)}, u32[]{:S(2)}) copy-start(bf16[1024,2048]{1,0:T(8,128)(2,1)} %constant.5.clone.table_ref) | copy-start | bytes 12582916

commit v6 on v5

--- a/solution.py
+++ b/solution.py
@@ -196,11 +196,12 @@
     phase = lax.broadcasted_iota(jnp.int32, (16, 128), 1) % 3
     total = jnp.where(phase == 0, triple, jnp.where(phase == 1, pltpu.roll(triple, 1, 1), pltpu.roll(triple, 2, 1)))
     amplitude = jnp.sqrt(total * (1.0 / 96) + 1e-06)
+    factor = own[0:1] / amplitude
+    xs[...] = (xs[...].reshape(16, 64, 128) * factor[:, None, :]).reshape(32, 32, 128)
     count_copy.wait()
     count = (jnp.sum(own, axis=1, keepdims=True) + jnp.sum(counts[1], axis=1, keepdims=True)) * (1.0 / 3)
-    weight = own / jnp.sqrt(jnp.round(count))
-    factor = weight[0:1] / amplitude
-    white[...] = (xs[...].reshape(16, 64, 128) * factor[:, None, :]).reshape(32, 32, 128).astype(BF16)
+    scale = jnp.broadcast_to(1.0 / jnp.sqrt(jnp.round(count)), (8, 128))[0:1]
+    white[...] = (xs[...] * scale[None]).astype(BF16)
 
     pl.semaphore_wait(core_sem, 1)
 
@@ -267,7 +268,8 @@
                 mixed = pltpu.roll(jnp.where(lane, im, re), 64, 1)
                 stage[pl.ds(512 * a + f, 16, stride=16), :] = jnp.where(lane, re, mixed)
                 stage[pl.ds(512 * a + 256 + f, 16, stride=16), :] = jnp.where(lane, mixed, im)
-        send[b] = jnp.stack([stage[pl.ds(512 * a, 512), :].reshape(2, 16, 16, 128).astype(BF16) for a in range(3)], axis=2)
+        for a in range(3):
+            send[b, :, :, a] = stage[pl.ds(512 * a, 512), :].reshape(2, 16, 16, 128).astype(BF16)
 
     def keep(b):
         target = stacks.at[b, slot] if b < 2 else last_ref.at[slot]

time: 50.8 us -> 50.8 us (level)
  no operation moved by 1% of the time
where the time goes in v6:
time: 50.8 us
  Pallas kernels  50.7 us (100%)
    pallas_call x1, Pallas kernels, stacked(): pl.pallas_call(stack_kernel, name='stack', out_shape=(pltpu.VMEM((32, 3,...  48.9 us
    pallas_call x1, Pallas kernels, to_lags(): pl.pallas_call(lag_kernel, name='lags', out_shape=jax.ShapeDtypeStruct((9...  1.85 us

profile of v6, /device:TPU:1, one launch (start us, length us, event | category | flops | bytes accessed | tf_op | source)
XLA Modules:
  0.0 50.8 jit_solution(3606983026540103458)
XLA Ops:
  0.0 0.0 copy-start
  0.0 48.9 %stack.1 = (bf16[32,3,16,128]{3,2,1,0:T(8,128)(2,1)S(1)}, bf16[2,3,64,2048]{3,2,1,0:T(8,128)(2,1)S(1)}) custom-call(f32[90,1,3000]{2,1,0:T(1,128)} %bitcast.4, s32[1,30]{1,0:T(1,128)} %av_hbm.1, bf16[4608,1024]{1,0:T(8,128)(2,1)} %constant.4.clone.table_hbm), custom_call_target="tpu_custom_call" | custom-call | tf_op jit(solution)/shard_map/stack/pallas_call | solution.py:321
  48.9 0.0 copy-done
  48.9 1.8 %lags.1 = bf16[9,64,2048]{2,1,0:T(8,128)(2,1)} custom-call(bf16[32,3,16,128]{3,2,1,0:T(8,128)(2,1)S(1)} %get-tuple-element.7.last_ref, bf16[2,3,64,2048]{3,2,1,0:T(8,128)(2,1)S(1)} %get-tuple-element.8.part_ref, bf16[1024,2048]{1,0:T(8,128)(2,1)S(1)} %copy-done), custom_call_target="tpu_custom_call" | custom-call | tf_op jit(solution)/shard_map/lags/pallas_call | solution.py:387
Async XLA Ops:
  0.0 48.9 %copy-start = (bf16[1024,2048]{1,0:T(8,128)(2,1)S(1)}, bf16[1024,2048]{1,0:T(8,128)(2,1)}, u32[]{:S(2)}) copy-start(bf16[1024,2048]{1,0:T(8,128)(2,1)} %constant.5.clone.table_ref) | copy-start | bytes 12582916

commit v7 on v6

--- a/solution.py
+++ b/solution.py
@@ -26,7 +26,7 @@
     key=lambda d: (-min(d[0], 4 - d[0]) - min(d[1], 4 - d[1]), (5 * d[0] + 3 * d[1] + d[2]) % 7),
 )
 SCHEDULE = (
-    ["P0", "F010", "P1", "F110", "F210", "L", "A01", "F021", "A11", "F121", "F310", "A21", "F221"]
+    ["P0", "F010", "P1", "F110", "F210", "A01", "F021", "A11", "F121", "F310", "L", "A21", "F221"]
     + ["A02", "F032", "F042", "A12", "F132", "F142", "A31", "F321", "A22", "F232", "F242"]
     + ["A03", "A13", "A04", "A14", "C0", "S00", "S01", "A32", "F332", "F342", "S02", "S03"]
     + ["A23", "A24", "C1", "S10", "S11", "S12", "S13"]

time: 50.8 us -> 50.8 us (level)
  no operation moved by 1% of the time
where the time goes in v7:
time: 50.8 us
  Pallas kernels  50.7 us (100%)
    pallas_call x1, Pallas kernels, stacked(): pl.pallas_call(stack_kernel, name='stack', out_shape=(pltpu.VMEM((32, 3,...  48.9 us
    pallas_call x1, Pallas kernels, to_lags(): pl.pallas_call(lag_kernel, name='lags', out_shape=jax.ShapeDtypeStruct((9...  1.85 us

profile of v7, /device:TPU:1, one launch (start us, length us, event | category | flops | bytes accessed | tf_op | source)
XLA Modules:
  0.0 50.8 jit_solution(11490498173662005989)
XLA Ops:
  0.0 0.0 copy-start
  0.0 48.9 %stack.1 = (bf16[32,3,16,128]{3,2,1,0:T(8,128)(2,1)S(1)}, bf16[2,3,64,2048]{3,2,1,0:T(8,128)(2,1)S(1)}) custom-call(f32[90,1,3000]{2,1,0:T(1,128)} %bitcast.4, s32[1,30]{1,0:T(1,128)} %av_hbm.1, bf16[4608,1024]{1,0:T(8,128)(2,1)} %constant.4.clone.table_hbm), custom_call_target="tpu_custom_call" | custom-call | tf_op jit(solution)/shard_map/stack/pallas_call | solution.py:321
  48.9 0.0 copy-done
  48.9 1.8 %lags.1 = bf16[9,64,2048]{2,1,0:T(8,128)(2,1)} custom-call(bf16[32,3,16,128]{3,2,1,0:T(8,128)(2,1)S(1)} %get-tuple-element.7.last_ref, bf16[2,3,64,2048]{3,2,1,0:T(8,128)(2,1)S(1)} %get-tuple-element.8.part_ref, bf16[1024,2048]{1,0:T(8,128)(2,1)S(1)} %copy-done), custom_call_target="tpu_custom_call" | custom-call | tf_op jit(solution)/shard_map/lags/pallas_call | solution.py:387
Async XLA Ops:
  0.0 48.9 %copy-start = (bf16[1024,2048]{1,0:T(8,128)(2,1)S(1)}, bf16[1024,2048]{1,0:T(8,128)(2,1)}, u32[]{:S(2)}) copy-start(bf16[1024,2048]{1,0:T(8,128)(2,1)} %constant.5.clone.table_ref) | copy-start | bytes 12582916
